TPU v7x, 32 devices: a whole 2x2x4 slice. The times are simulated.
32 devices in a mesh: grp: 16 (over z, x, core), tp: 2 (over y).
Axes of the slice: x: 2, y: 2, z: 4, core: 2. Of those that a mesh axis runs over, the one named last changes fastest.
Arguments:
- kv_weight: bfloat16 [8192, 2048], P('tp'), may hold values from -0.0625 to 0.0625
- kv_bias: bfloat16 [2048], P('tp'), may hold values from -3 to 3
- hidden_in: bfloat16 [4, 16, 32, 8192], P(None, 'grp', None, 'tp'), may hold values from -6 to 6
- queries: bfloat16 [4, 16, 32, 8192], P(None, 'grp', None, 'tp'), may hold values from -139 to 139
- res_cache: bfloat16 [16, 16, 128, 2048], P('grp', None, None, 'tp'), may hold values from -6 to 6
- res_len: int32 [16, 16], P('grp'), may hold values from 1 to 128, 1088 in all within a row
- long_cache: bfloat16 [16, 16, 512, 2048], P('grp', None, None, 'tp'), may hold values from -6 to 6
- long_len: int32 [16, 16], replicated, may hold values from 1 to 512, 4096 in all within a row
- long_dest: int32 [16, 16], replicated, may hold values from 0 to 15, each once within a row
Outputs:
- attention_out: bfloat16 [4, 16, 32, 8192], P(None, 'grp', None, 'tp')
Inputs may be any that keep to these rules, and one draw needn't show every extreme that they name: `res_len`: each group's lengths sum to 1088, and the largest is 128. `long_len`: each home group's lengths sum to 4096, and the largest is 512. `long_dest`: each row is a permutation of the groups, so every group sends one request to every group and receives one from every group.
All inputs are finite; a program needn't handle non-finite values.
Results may differ from a plain program's by a relative error of at most 0.0051.
Values may be sent and summed in bfloat16 or wider, within the bound.
No kernel may reach another device: no remote copies, remote signals or barrier semaphores. Data moves between devices by JAX's collectives and lax.ppermute only.
A program may use at most 192 MiB of HBM per device.

v0:
```python
import jax
import jax.numpy as jnp
from jax import lax
from jax.sharding import PartitionSpec as P

HS = 128


ROPE_BASE = 1000000.0
masked_score = -1e30


def rotate(keys_raw, positions):
    half_dim = HS // 2
    freqs = jnp.power(jnp.float32(ROPE_BASE), -2.0 * jnp.arange(half_dim, dtype=jnp.float32) / HS)
    angles = positions.astype(jnp.float32)[..., None] * freqs
    cosine = jnp.cos(angles)
    sine = jnp.sin(angles)
    first_half = keys_raw[..., :half_dim]
    second_half = keys_raw[..., half_dim:]
    return jnp.concatenate(
        [first_half * cosine - second_half * sine, second_half * cosine + first_half * sine],
        axis=-1,
    )


def attend(query, cache, lengths, new_keys, new_values):
    kv_heads = new_keys.shape[2]
    capacity = cache.shape[1]
    cache = cache.reshape(cache.shape[0], capacity, kv_heads, 2 * HS)
    old_keys = cache[..., :HS]
    old_values = cache[..., HS:]
    scale = HS ** (-0.5)
    scores_old = (
        jnp.einsum("sbkqd,bckd->sbkqc", query, old_keys, preferred_element_type=jnp.float32) * scale
    )
    valid = jnp.arange(capacity, dtype=jnp.int32)[None, :] < lengths[:, None]
    scores_old = jnp.where(valid[None, :, None, None, :], scores_old, masked_score)
    scores_new = (
        jnp.einsum("sbkqd,tbkd->sbkqt", query, new_keys, preferred_element_type=jnp.float32) * scale
    )
    step_count = new_keys.shape[0]
    causal = jnp.arange(step_count)[None, :] <= jnp.arange(step_count)[:, None]
    scores_new = jnp.where(causal[:, None, None, None, :], scores_new, masked_score)
    highest = jnp.maximum(jnp.max(scores_old, -1), jnp.max(scores_new, -1))[..., None]
    probs_old = jnp.exp(scores_old - highest)
    probs_new = jnp.exp(scores_new - highest)
    total = jnp.sum(probs_old, -1, keepdims=True) + jnp.sum(probs_new, -1, keepdims=True)
    weights_old = (probs_old / total).astype(jnp.bfloat16)
    weights_new = (probs_new / total).astype(jnp.bfloat16)
    mixed = jnp.einsum(
        "sbkqc,bckd->sbkqd", weights_old, old_values, preferred_element_type=jnp.float32
    )
    mixed = mixed + jnp.einsum(
        "sbkqt,tbkd->sbkqd", weights_new, new_values, preferred_element_type=jnp.float32
    )
    return mixed.astype(jnp.bfloat16)


def per_device(
    kv_weight, kv_bias, hidden_in, queries, res_cache, res_len, long_cache, long_len, long_dest
):
    step_count, _, serve_rows, width_part = hidden_in.shape
    kv_cols = kv_bias.shape[0]
    kv_heads = kv_cols // (2 * HS)
    head_count = queries.shape[3] // HS
    staying_count = res_cache.shape[1]
    local_weight = lax.all_to_all(kv_weight, "tp", split_axis=1, concat_axis=0, tiled=True)
    piece = lax.all_gather(hidden_in, "tp", axis=3, tiled=True)
    flat_piece = piece.reshape(step_count * serve_rows, piece.shape[3])
    kv_raw = jnp.dot(flat_piece, local_weight, preferred_element_type=jnp.float32)
    kv_raw = kv_raw + kv_bias.astype(jnp.float32)
    kv_raw = kv_raw.reshape(step_count, serve_rows, kv_heads, 2 * HS)
    group_index = lax.axis_index("grp")
    matched = (long_dest == group_index).astype(jnp.int32)
    len_in = jnp.sum(matched * long_len, axis=1)
    own_len = res_len[0]
    served_len = jnp.concatenate([own_len, len_in])
    positions = served_len[None, :] + jnp.arange(step_count, dtype=jnp.int32)[:, None]
    new_keys = rotate(kv_raw[..., :HS], positions[:, :, None]).astype(jnp.bfloat16)
    new_values = kv_raw[..., HS:].astype(jnp.bfloat16)
    query = queries[:, 0].reshape(step_count, serve_rows, kv_heads, head_count // kv_heads, HS)
    staying = attend(
        query[:, :staying_count],
        res_cache[0],
        own_len,
        new_keys[:, :staying_count],
        new_values[:, :staying_count],
    )
    own_dest = lax.dynamic_index_in_dim(long_dest, group_index, 0, keepdims=False)
    order = jnp.argsort(own_dest)
    outgoing = long_cache[0][order]
    arrived = lax.all_to_all(outgoing, "grp", split_axis=0, concat_axis=0, tiled=True)
    moving = attend(
        query[:, staying_count:],
        arrived,
        len_in,
        new_keys[:, staying_count:],
        new_values[:, staying_count:],
    )
    joined = jnp.concatenate([staying, moving], axis=1)
    return joined.reshape(step_count, 1, serve_rows, head_count * HS)


def solution(mesh):
    placed = (
        P("tp", None),
        P("tp"),
        P(None, "grp", None, "tp"),
        P(None, "grp", None, "tp"),
        P("grp", None, None, "tp"),
        P("grp", None),
        P("grp", None, None, "tp"),
        P(),
        P(),
    )
    return jax.shard_map(
        per_device,
        mesh=mesh,
        in_specs=placed,
        out_specs=P(None, "grp", None, "tp"),
        check_vma=False,
    )
```

profile of v0, /device:TPU:11, one launch (start us, length us, event | category | flops | bytes accessed | tf_op | source)
XLA Modules:
  0.0 631.2 jit_solution(15882831497844384874)
XLA Ops:
  6.5 20.7 %copy.28 = bf16[4096,2048]{0,1:T(8,128)(2,1)} copy(bf16[4096,2048]{1,0:T(8,128)(2,1)} %param.9) | data formatting | bytes 33554432 | tf_op args[0]
  27.3 0.0 copy-start.3
  27.3 9.8 %all-to-all-start = ((bf16[4096,2,1024]{0,2,1:T(8,128)(2,1)}), bf16[4096,2,1024]{0,2,1:T(8,128)(2,1)}, u32[]{:S(2)}, u32[]{:S(2)}) async-start(bf16[4096,2,1024]{0,2,1:T(8,128)(2,1)} %bitcast.111), calls=%async_computation | async-start | bytes 33554432 | tf_op jit(solution)/shard_map/all_to_all | solution.py:68
  37.1 0.0 copy-done.3
  37.1 1.2 sort.17
  38.4 13.0 %gather_fusion = bf16[16,512,1024]{2,1,0:T(8,128)(2,1)} fusion(bf16[16,512,1024]{2,1,0:T(8,128)(2,1)} %bitcast.112, s32[1024]{0:T(1024)S(1)} %pad_clamp_fusion), kind=kCustom, calls=%fused_computation | custom fusion | bytes 33554496 | tf_op jit(solution)/shard_map/gather | solution.py:92
  51.4 0.0 copy-start.5
  51.4 0.0 copy-start.1
  51.4 167.3 %all-to-all-done = bf16[4096,2,1024]{0,2,1:T(8,128)(2,1)} async-done(((bf16[4096,2,1024]{0,2,1:T(8,128)(2,1)}), bf16[4096,2,1024]{0,2,1:T(8,128)(2,1)}, u32[]{:S(2)}, u32[]{:S(2)}) %all-to-all-start) | async-done | bytes 16777248 | tf_op jit(solution)/shard_map/all_to_all | solution.py:68
  218.7 7.4 %all-to-all-start.1 = ((bf16[16,512,1024]{2,1,0:T(8,128)(2,1)}), bf16[16,512,1024]{2,1,0:T(8,128)(2,1)}, u32[]{:S(2)}, u32[]{:S(2)}) async-start(bf16[16,512,1024]{2,1,0:T(8,128)(2,1)} %gather_fusion), calls=%async_computation.1 | async-start | bytes 33554432 | tf_op jit(solution)/shard_map/all_to_all | solution.py:93
  226.1 0.0 all-gather.2.cloned.1.call-start
  226.2 0.7 all-gather.2.cloned.1.call-update
  226.8 0.0 copy-done.5
  226.9 0.0 copy-done.1
  226.9 0.2 copy.54
  227.1 0.0 copy-start.4
  227.1 0.0 copy-start.6
  227.2 6.6 %copy.25 = bf16[1,16,128,1024]{2,3,1,0:T(8,128)(2,1)} copy(bf16[1,16,128,1024]{3,2,1,0:T(8,128)(2,1)} %param.13) | data formatting | bytes 8388608 | tf_op args[4]
  233.8 0.0 copy-done.4
  233.8 0.1 select_reduce_fusion
  233.9 0.0 copy-done.6
  233.9 0.1 pad_add_fusion
  234.0 0.1 iota_compare_fusion.1
  234.0 0.1 iota_compare_fusion
  234.1 0.1 add_convert_fusion.1
  234.2 0.5 multiply_cosine_fusion
  234.7 0.1 fusion.46
  234.8 3.2 fusion.48
  238.1 21.3 %copy.29 = bf16[2,4096,1024]{2,1,0:T(8,128)(2,1)} copy(bf16[2,4096,1024]{1,2,0:T(8,128)(2,1)} %bitcast.7) | data formatting | bytes 33554432 | tf_op jit(solution)/shard_map/all_to_all | solution.py:68
  259.4 1.9 all-gather.2.cloned.1.call-done
  261.3 8.7 %convolution_add_fusion.1 = f32[128,1024]{1,0:T(8,128)S(1)} fusion(bf16[128,8192]{1,0:T(8,128)(2,1)} %bitcast.118, bf16[8192,1024]{1,0:T(8,128)(2,1)} %bitcast.110, f32[1024]{0:T(1024)S(1)} %convert_element_type.36), kind=kOutput, calls=%fused_computation.36 | convolution fusion | flops 2147614720 | bytes 19402752 | tf_op jit(solution)/shard_map/dot_general | solution.py:71
  270.0 0.2 reshape.127
  270.3 0.0 copy-start.2
  270.3 0.3 copy.30
  270.7 0.0 copy-start
  270.7 0.3 copy.64
  271.0 0.2 subtract_convert_fusion
  271.3 2.5 fusion.49
  273.7 0.0 copy-done.2
  273.8 0.5 fusion.30
  274.3 0.8 fusion.23
  275.1 2.5 fusion.47
  277.6 0.0 copy-done
  277.6 1.4 fusion.11
  279.0 0.5 fusion.17
  279.5 308.7 %all-to-all-done.1 = bf16[16,512,1024]{2,1,0:T(8,128)(2,1)} async-done(((bf16[16,512,1024]{2,1,0:T(8,128)(2,1)}), bf16[16,512,1024]{2,1,0:T(8,128)(2,1)}, u32[]{:S(2)}, u32[]{:S(2)}) %all-to-all-start.1) | async-done | bytes 16777248 | tf_op jit(solution)/shard_map/all_to_all | solution.py:93
  588.2 21.6 %copy.34 = bf16[16,512,1024]{1,2,0:T(8,128)(2,1)} copy(bf16[16,512,1024]{2,1,0:T(8,128)(2,1)} %all-to-all-done.1) | data formatting | bytes 33554432 | tf_op jit(solution)/shard_map/all_to_all | solution.py:93
  609.8 4.6 bitcast_reduce_fusion
  614.5 0.5 fusion.31
  615.0 2.0 fusion.3
  617.0 5.2 fusion.1
  622.3 0.5 fusion.18
  622.8 0.1 pad_maximum_fusion
  622.9 0.2 copy.38
  623.1 1.3 reshape.129
  (11 shorter events, 0.2 us)
Async XLA Ops:
  27.3 9.8 %copy-start.3 = (s32[16,16]{1,0:T(8,128)S(1)}, s32[16,16]{1,0:T(8,128)}, u32[]{:S(2)}) copy-start(s32[16,16]{1,0:T(8,128)} %param.17) | copy-start | bytes 3076
  27.3 191.4 %all-to-all-start = ((bf16[4096,2,1024]{0,2,1:T(8,128)(2,1)}), bf16[4096,2,1024]{0,2,1:T(8,128)(2,1)}, u32[]{:S(2)}, u32[]{:S(2)}) async-start(bf16[4096,2,1024]{0,2,1:T(8,128)(2,1)} %bitcast.111), calls=%async_computation | async-start | bytes 33554432 | tf_op jit(solution)/shard_map/all_to_all | solution.py:68
  51.4 175.5 %copy-start.5 = (bf16[1024]{0:T(1024)(128)(2,1)S(1)}, bf16[1024]{0:T(1024)(128)(2,1)}, u32[]{:S(2)}) copy-start(bf16[1024]{0:T(1024)(128)(2,1)} %param.10) | copy-start | bytes 6148
  51.4 175.5 %copy-start.1 = (bf16[4,1,32,4096]{3,2,1,0:T(8,128)(2,1)S(1)}, bf16[4,1,32,4096]{3,2,1,0:T(8,128)(2,1)}, u32[]{:S(2)}) copy-start(bf16[4,1,32,4096]{3,2,1,0:T(8,128)(2,1)} %param.12) | copy-start | bytes 3145732
  218.7 369.5 %all-to-all-start.1 = ((bf16[16,512,1024]{2,1,0:T(8,128)(2,1)}), bf16[16,512,1024]{2,1,0:T(8,128)(2,1)}, u32[]{:S(2)}, u32[]{:S(2)}) async-start(bf16[16,512,1024]{2,1,0:T(8,128)(2,1)} %gather_fusion), calls=%async_computation.1 | async-start | bytes 33554432 | tf_op jit(solution)/shard_map/all_to_all | solution.py:93
  226.1 35.2 %all-gather.2.cloned.1.call-start = ((), (), s32[]{:S(2)}) async-start(), calls=%async_computation.2 | async-start | bytes 3145728 | tf_op jit(solution)/shard_map/all_gather | solution.py:69
  227.1 6.6 %copy-start.4 = (s32[16,16]{1,0:T(8,128)S(1)}, s32[16,16]{1,0:T(8,128)}, u32[]{:S(2)}) copy-start(s32[16,16]{1,0:T(8,128)} %param.16) | copy-start | bytes 3076
  227.1 6.7 %copy-start.6 = (s32[1,16]{1,0:T(1,128)S(1)}, s32[1,16]{1,0:T(1,128)}, u32[]{:S(2)}) copy-start(s32[1,16]{1,0:T(1,128)} %param.14) | copy-start | bytes 196
  270.3 3.4 copy-start.2
  270.7 6.9 %copy-start = (bf16[1,16,128,1024]{2,3,1,0:T(8,128)(2,1)S(1)}, bf16[1,16,128,1024]{2,3,1,0:T(8,128)(2,1)}, u32[]{:S(2)}) copy-start(bf16[1,16,128,1024]{2,3,1,0:T(8,128)(2,1)} %copy.25) | copy-start | bytes 12582916
Sparse Core Ops, SparseCore 0:
  228.5 32.7 all-gather.1
where the time goes:
time: 633 us; the launch traced here: 631 us
  waiting for transfers between devices  479 us (76%)
  local copies, waits for them, and re-layouts  86 us (14%)
  matrix products  29.2 us (5%)
  starting transfers between devices  17.3 us (3%)
  between operations  13.7 us (2%)
  other arithmetic  6.51 us (1%)
    all_to_all x1, waiting for transfers between devices, per_device(): lax.all_to_all(outgoing, 'grp', split_axis=0, concat_axis=0, tiled=True)  309 us
    all_to_all x1, waiting for transfers between devices, per_device(): lax.all_to_all(kv_weight, 'tp', split_axis=1, concat_axis=0, tiled=True)  167 us
    unnamed x17, local copies, waits for them, and re-layouts  27.6 us
    all_to_all x1, local copies, waits for them, and re-layouts, per_device(): lax.all_to_all(outgoing, 'grp', split_axis=0, concat_axis=0, tiled=True)  21.6 us
    all_to_all x1, local copies, waits for them, and re-layouts, per_device(): lax.all_to_all(kv_weight, 'tp', split_axis=1, concat_axis=0, tiled=True)  21.3 us
    gather x1, local copies, waits for them, and re-layouts, per_device(): outgoing = long_cache[0][order]  13 us
  transfers between devices with their start and end apart: 3, of which 3 were waited for; matrix products, arithmetic and copies ran while one was open for 10% of the time, Pallas kernels for 0%

commit v1 on v0

v1 whole, which is shorter than its diff:
```python
import jax
import jax.numpy as jnp
from jax import lax
from jax.sharding import PartitionSpec as P

HS = 128


ROPE_BASE = 1000000.0
masked_score = -1e30


def rotate(keys_raw, positions):
    half_dim = HS // 2
    freqs = jnp.power(jnp.float32(ROPE_BASE), -2.0 * jnp.arange(half_dim, dtype=jnp.float32) / HS)
    angles = positions.astype(jnp.float32)[..., None] * freqs
    cosine = jnp.cos(angles)
    sine = jnp.sin(angles)
    first_half = keys_raw[..., :half_dim]
    second_half = keys_raw[..., half_dim:]
    return jnp.concatenate(
        [first_half * cosine - second_half * sine, second_half * cosine + first_half * sine],
        axis=-1,
    )


def attend_old(query, cache, lengths):
    rows, capacity, cols = cache.shape
    kv_heads = cols // (2 * HS)
    cache = cache.reshape(rows, capacity, kv_heads, 2 * HS)
    scores = jnp.einsum(
        "bknd,bckd->bknc", query, cache[..., :HS], preferred_element_type=jnp.float32
    ) * HS ** (-0.5)
    valid = jnp.arange(capacity, dtype=jnp.int32)[None, :] < lengths[:, None]
    scores = jnp.where(valid[:, None, None, :], scores, masked_score)
    highest = jnp.max(scores, -1, keepdims=True)
    probs = jnp.exp(scores - highest)
    total = jnp.sum(probs, -1, keepdims=True)
    weights = (probs / total).astype(jnp.bfloat16)
    mixed = jnp.einsum(
        "bknc,bckd->bknd", weights, cache[..., HS:], preferred_element_type=jnp.float32
    )
    return mixed, (highest + jnp.log(total))[..., 0]


def per_device(
    kv_weight, kv_bias, hidden_in, queries, res_cache, res_len, long_cache, long_len, long_dest
):
    step_count, _, serve_rows, width_part = hidden_in.shape
    kv_cols = kv_bias.shape[0]
    kv_heads = kv_cols // (2 * HS)
    head_count = queries.shape[3] // HS
    per_kv = head_count // kv_heads
    staying = res_cache.shape[1]
    moving = serve_rows - staying
    tp_size = lax.axis_size("tp")
    tp_index = lax.axis_index("tp")
    group_index = lax.axis_index("grp")
    query = queries[:, 0].reshape(step_count, serve_rows, kv_heads, per_kv, HS)
    query = jnp.transpose(query, (1, 2, 0, 3, 4)).reshape(
        serve_rows, kv_heads, step_count * per_kv, HS
    )
    asked = lax.all_to_all(query[staying:], "grp", split_axis=0, concat_axis=0, tiled=True)

    flat_hidden = hidden_in.reshape(step_count * serve_rows, width_part)
    partial = jnp.dot(flat_hidden, kv_weight, preferred_element_type=jnp.float32)
    kv_raw = lax.dynamic_slice_in_dim(partial, tp_index * kv_cols, kv_cols, axis=1)
    for shift in range(1, tp_size):
        other = lax.rem(tp_index + shift, tp_size)
        piece = lax.dynamic_slice_in_dim(partial, other * kv_cols, kv_cols, axis=1)
        kv_raw = kv_raw + lax.ppermute(
            piece, "tp", [(i, (i + shift) % tp_size) for i in range(tp_size)]
        )

    own_dest = lax.dynamic_index_in_dim(long_dest, group_index, 0, keepdims=False)
    home_len = lax.dynamic_index_in_dim(long_len, group_index, 0, keepdims=False)
    mixed, lse = attend_old(asked[own_dest], long_cache[0], home_len)
    back = jnp.argsort(own_dest)
    lse_hi = lse.astype(jnp.bfloat16)
    rest = lse - lse_hi.astype(jnp.float32)
    lse_mid = rest.astype(jnp.bfloat16)
    lse_lo = (rest - lse_mid.astype(jnp.float32)).astype(jnp.bfloat16)
    count = kv_heads * step_count * per_kv
    answer = jnp.concatenate(
        [mixed.astype(jnp.bfloat16).reshape(moving, -1)]
        + [x.reshape(moving, count) for x in (lse_hi, lse_mid, lse_lo)],
        axis=1,
    )[back]
    answer = lax.all_to_all(answer, "grp", split_axis=0, concat_axis=0, tiled=True)
    moved = answer[:, : count * HS].astype(jnp.float32).reshape(moving, kv_heads, -1, HS)
    stats = answer[:, count * HS :].astype(jnp.float32).reshape(moving, 3, kv_heads, -1)
    moved_lse = stats[:, 0] + stats[:, 1] + stats[:, 2]

    kv_raw = kv_raw + kv_bias.astype(jnp.float32)
    kv_raw = kv_raw.reshape(step_count, serve_rows, kv_heads, 2 * HS)
    matched = (long_dest == group_index).astype(jnp.int32)
    len_in = jnp.sum(matched * long_len, axis=1)
    own_len = res_len[0]
    served_len = jnp.concatenate([own_len, len_in])
    positions = served_len[None, :] + jnp.arange(step_count, dtype=jnp.int32)[:, None]
    new_keys = rotate(kv_raw[..., :HS], positions[:, :, None]).astype(jnp.bfloat16)
    new_values = kv_raw[..., HS:].astype(jnp.bfloat16)

    stayed, stayed_lse = attend_old(query[:staying], res_cache[0], own_len)
    old = jnp.concatenate([stayed, moved], axis=0)
    old_lse = jnp.concatenate([stayed_lse, moved_lse], axis=0)
    scores_new = jnp.einsum(
        "bknd,tbkd->bknt", query, new_keys, preferred_element_type=jnp.float32
    ) * HS ** (-0.5)
    causal = jnp.arange(step_count)[None, :] <= (jnp.arange(step_count * per_kv) // per_kv)[:, None]
    scores_new = jnp.where(causal, scores_new, masked_score)
    highest = jnp.maximum(old_lse, jnp.max(scores_new, -1))[..., None]
    share_old = jnp.exp(old_lse[..., None] - highest)
    probs_new = jnp.exp(scores_new - highest)
    total = share_old + jnp.sum(probs_new, -1, keepdims=True)
    weights_new = (probs_new / total).astype(jnp.bfloat16)
    joined = old * (share_old / total) + jnp.einsum(
        "bknt,tbkd->bknd", weights_new, new_values, preferred_element_type=jnp.float32
    )
    joined = joined.astype(jnp.bfloat16).reshape(serve_rows, kv_heads, step_count, per_kv, HS)
    joined = jnp.transpose(joined, (2, 0, 1, 3, 4))
    return joined.reshape(step_count, 1, serve_rows, head_count * HS)


def solution(mesh):
    placed = (
        P("tp", None),
        P("tp"),
        P(None, "grp", None, "tp"),
        P(None, "grp", None, "tp"),
        P("grp", None, None, "tp"),
        P("grp", None),
        P("grp", None, None, "tp"),
        P(),
        P(),
    )
    return jax.shard_map(
        per_device,
        mesh=mesh,
        in_specs=placed,
        out_specs=P(None, "grp", None, "tp"),
        check_vma=False,
    )
```

time: 633 us -> 107 us (0.17)
  the two profiles are of different devices: /device:TPU:11 before, /device:TPU:0 now
where the time goes in v1:
time: 107 us; the launch traced here: 106 us
  local copies, waits for them, and re-layouts  43.4 us (41%)
  matrix products  26.3 us (25%)
  starting transfers between devices  14.9 us (14%)
  waiting for transfers between devices  11.3 us (11%)
  other arithmetic  9.64 us (9%)
    unnamed x26, local copies, waits for them, and re-layouts  34.7 us
    all_to_all x1, waiting for transfers between devices, per_device(): lax.all_to_all(answer, 'grp', split_axis=0, concat_axis=0, tiled=True)  11.3 us
    dot_general x1, matrix products, per_device(): jnp.dot(flat_hidden, kv_weight, preferred_element_type=jnp.float32)  8.18 us
    dot_general x2, matrix products, attend_old(): jnp.einsum('bknc,bckd->bknd', weights, cache[..., HS:], preferred_element...  7.64 us
    dot_general x2, matrix products, attend_old(): jnp.einsum('bknd,bckd->bknc', query, cache[..., :HS], preferred_element_t...  7.45 us
    all_to_all x1, starting transfers between devices, per_device(): lax.all_to_all(answer, 'grp', split_axis=0, concat_axis=0, tiled=True)  5.99 us
    all_to_all x1, starting transfers between devices, per_device(): lax.all_to_all(query[staying:], 'grp', split_axis=0, concat_axis=0, tiled...  5.97 us
    ppermute x1, starting transfers between devices, per_device(): lax.ppermute(piece, 'tp', [(i, (i + shift) % tp_size) for i in range(tp_s...  2.97 us
  transfers between devices with their start and end apart: 3, of which 1 were waited for; matrix products, arithmetic and copies ran while one was open for 59% of the time, Pallas kernels for 0%

profile of v1, /device:TPU:0, one launch (start us, length us, event | category | flops | bytes accessed | tf_op | source)
XLA Modules:
  0.0 106.0 jit_solution(9883701861415599755)
XLA Ops:
  0.0 0.0 copy-start
  0.0 1.2 %copy-done = bf16[4,1,32,4096]{3,2,1,0:T(8,128)(2,1)S(1)} copy-done((bf16[4,1,32,4096]{3,2,1,0:T(8,128)(2,1)S(1)}, bf16[4,1,32,4096]{3,2,1,0:T(8,128)(2,1)}, u32[]{:S(2)}) %copy-start) | copy-done | bytes 1048600
  1.2 8.2 %fusion.57 = f32[128,2048]{1,0:T(8,128)S(1)} fusion(bf16[128,4096]{1,0:T(8,128)(2,1)S(1)} %bitcast.83, bf16[4096,2048]{1,0:T(8,128)(2,1)} %param.9), kind=kOutput, calls=%fused_computation.103 | convolution fusion | flops 2147483648 | bytes 18874368 | tf_op jit(solution)/shard_map/dot_general | solution.py:66
  9.4 0.0 copy-start.5
  9.4 0.0 copy-start.6
  9.4 0.0 copy-start.8
  9.5 0.9 constant_dynamic-slice_fusion
  10.3 3.0 %collective-permute-start = (f32[128,1024]{1,0:T(8,128)}, f32[128,1024]{1,0:T(8,128)}, u32[]{:S(2)}, u32[]{:S(2)}) collective-permute-start(f32[128,1024]{1,0:T(8,128)} %constant_dynamic-slice_fusion), channel_id=1, source_target_pairs={{0,1},{1,0},{2,3},{3,2},{4,5},{5,4},{6,7},{7,6},{8,9},{9,8},{10,11... | collective-permute-start | bytes 1572872 | tf_op jit(solution)/shard_map/ppermute | solution.py:71
  13.3 0.0 copy-done.3
  13.3 0.2 copy.73
  13.5 0.3 copy.91
  13.8 0.9 slice_bitcast_fusion
  14.7 6.0 %all-to-all-start = ((bf16[16,4,32,128]{3,2,1,0:T(8,128)(2,1)}), bf16[16,4,32,128]{3,2,1,0:T(8,128)(2,1)}, u32[]{:S(2)}, u32[]{:S(2)}) async-start(bf16[16,4,32,128]{3,2,1,0:T(8,128)(2,1)} %slice_bitcast_fusion), calls=%async_computation | async-start | bytes 1048576 | tf_op jit(solution)/shard_map/all_to_all | solution.py:63
  20.7 0.0 copy-done.5
  20.7 0.0 copy-done.6
  20.7 0.1 select_reduce_fusion
  20.9 1.2 %sort.17 = (s32[16]{0:T(128)}, s32[16]{0:T(128)S(1)}) sort(s32[16]{0:T(128)S(1)} %fusion.47, s32[16]{0:T(128)S(1)} %iota.42), dimensions={0}, to_apply=%region_4.5 | sort | flops 64 | bytes 256 | tf_op jit(solution)/shard_map/jit(argsort)/sort | solution.py:78
  22.1 0.0 copy-done.8
  22.1 0.1 iota_compare_fusion.1
  22.2 0.1 and_select_fusion
  22.3 0.1 iota_compare_fusion
  22.4 0.1 add_convert_fusion.1
  22.5 6.4 %copy.48 = bf16[1,16,128,1024]{2,3,1,0:T(8,128)(2,1)} copy(bf16[1,16,128,1024]{3,2,1,0:T(8,128)(2,1)} %param.13) | data formatting | bytes 8388608 | tf_op args[4]
  28.9 21.6 %copy.51 = bf16[1,16,512,1024]{2,3,1,0:T(8,128)(2,1)} copy(bf16[1,16,512,1024]{3,2,1,0:T(8,128)(2,1)} %param.15) | data formatting | bytes 33554432 | tf_op args[6]
  50.5 2.5 %fusion.55 = (f32[16,4,32]{2,1,0:T(4,128)S(1)}, f32[16,4,32,128]{3,2,1,0:T(8,128)S(1)}) fusion(bf16[16,128,4,256]{1,3,2,0:T(8,128)(2,1)} %bitcast.86, bf16[32,4,4,8,128]{4,3,2,1,0:T(8,128)(2,1)S(1)} %bitcast.91, pred[16,128]{1,0:T(8,128)(4,1)S(1)} %iota_compare_fusion.1), kind=kOutput, calls=%fused_computation.101 | convolution fusion | flops 67893248 | bytes 3680256 | tf_op jit(solution)/shard_map/bknd,bckd->bknc/dot_general | solution.py:31
  53.0 0.7 fusion.30
  53.7 0.5 multiply_cosine_fusion
  54.2 0.0 copy-done.2
  54.2 2.2 %fusion.6 = f32[16,4,32,128]{3,2,1,0:T(8,128)} fusion(bf16[16,128,4,256]{1,3,2,0:T(8,128)(2,1)S(1)} %bitcast.87, f32[16,4,32,128]{3,2,1,0:T(8,128)S(1)} %get-tuple-element.21, f32[16,4,32]{2,1,0:T(4,128)S(1)} %fusion.30, f32[16,4,32]{2,1,0:T(4,128)S(1)} %get-tuple-element.20), kind=kOutput, calls=%fused_computation.11 | convolution fusion | flops 67895296 | bytes 4259840 | tf_op jit(solution)/shard_map/bknc,bckd->bknd/dot_general | solution.py:40
  56.5 0.0 all-to-all-done
  56.5 1.7 %gather_fusion = bf16[16,4,32,128]{3,2,1,0:T(8,128)(2,1)S(1)} fusion(bf16[16,4,32,128]{3,2,1,0:T(8,128)(2,1)} %all-to-all-done, s32[1024]{0:T(1024)S(1)} %pad_clamp_fusion.1), kind=kCustom, calls=%fused_computation | custom fusion | bytes 1048640 | tf_op jit(solution)/shard_map/gather | solution.py:77
  58.2 4.9 %fusion.4 = (f32[16,4,32]{2,1,0:T(4,128)S(1)}, f32[16,4,32,512]{3,2,1,0:T(8,128)S(1)}) fusion(pred[16,512]{1,0:T(8,128)(4,1)S(1)} %iota_compare_fusion, bf16[16,4,32,128]{3,2,1,0:T(8,128)(2,1)S(1)} %gather_fusion, bf16[16,512,4,256]{1,3,2,0:T(8,128)(2,1)} %bitcast.84), kind=kOutput, calls=%fused_computation.9 | convolution fusion | flops 271579136 | bytes 13123584 | tf_op jit(solution)/shard_map/bknd,bckd->bknc/dot_general | solution.py:31
  63.1 1.6 %fusion.5 = f32[16,4,32]{2,1,0:T(4,128)S(1)} fusion(f32[16,4,32,512]{3,2,1,0:T(8,128)S(1)} %get-tuple-element.19, f32[16,4,32]{2,1,0:T(4,128)S(1)} %get-tuple-element.18, pred[16,512]{1,0:T(8,128)(4,1)S(1)} %iota_compare_fusion), kind=kLoop, calls=%fused_computation.10 | loop fusion | flops 4192256 | bytes 4218880 | tf_op jit(solution)/shard_map/reduce_sum | solution.py:38
  64.8 5.4 %fusion.24 = bf16[16,4,32,128]{3,2,1,0:T(8,128)(2,1)S(1)} fusion(bf16[16,512,4,256]{1,3,2,0:T(8,128)(2,1)} %bitcast.85, f32[16,4,32,512]{3,2,1,0:T(8,128)S(1)} %get-tuple-element.19, f32[16,4,32]{2,1,0:T(4,128)S(1)} %fusion.5, f32[16,4,32]{2,1,0:T(4,128)S(1)} %get-tuple-element.18, pred[16,512]{1,0:T(8,128)(4,1)S(1)} %iota_compare_fusion), kind=kOutput, calls=%fused_computation.26 | convolution fusion | flops 273940480 | bytes 13131776 | tf_op jit(solution)/shard_map/bknc,bckd->bknd/dot_general | solution.py:40
  70.2 1.1 %copy.93 = bf16[2,8,128,128]{3,1,2,0:T(8,128)(2,1)} copy(bf16[2,8,128,128]{3,2,1,0:T(8,128)(2,1)S(1)} %bitcast.98) | data formatting | bytes 1048576
  71.3 0.1 add.118
  71.4 1.1 %pad_maximum_fusion = bf16[16,16768]{1,0:T(8,128)(2,1)S(1)} fusion(bf16[16,128]{1,0:T(8,128)(2,1)S(1)} %get-tuple-element.16, bf16[16,128]{1,0:T(8,128)(2,1)S(1)} %get-tuple-element.17, bf16[16,128]{1,0:T(8,128)(2,1)S(1)} %get-tuple-element.15, bf16[16,16384]{1,0:T(8,128)(2,1)} %bitcast.95), kind=kLoop, calls=%fused_computation.37 | loop fusion | flops 2146304 | bytes 1073152 | tf_op jit(solution)/shard_map/concatenate | solution.py:84
  72.5 0.0 copy-start.7
  72.5 1.7 %gather_fusion.1 = bf16[16,16768]{1,0:T(8,128)(2,1)} fusion(bf16[16,16768]{1,0:T(8,128)(2,1)S(1)} %pad_maximum_fusion, s32[1024]{0:T(1024)S(1)} %pad_clamp_fusion), kind=kCustom, calls=%fused_computation.1 | custom fusion | bytes 1073216 | tf_op jit(solution)/shard_map/gather | solution.py:84
  74.2 0.5 broadcast.143
  74.7 2.0 %reduce = bf16[16,16768]{1,0:T(8,128)(2,1)S(1)} reduce(bf16[16,1,16768]{2,0,1:T(8,128)(2,1)} %bitcast.92, bf16[]{:T(256)} %broadcast.143), dimensions={1}, to_apply=%copy.54.reduce_sub_computation | reduce | bytes 1073154 | tf_op jit(solution)/shard_map/all_to_all | solution.py:89
  76.7 1.3 %reshape.284 = bf16[16,2,8384]{2,1,0:T(2,128)(2,1)} reshape(bf16[16,16768]{1,0:T(8,128)(2,1)S(1)} %reduce) | data formatting | bytes 1073152
  78.1 6.0 %all-to-all-start.1 = ((bf16[16,2,8384]{2,1,0:T(2,128)(2,1)}), bf16[16,2,8384]{2,1,0:T(2,128)(2,1)}, u32[]{:S(2)}, u32[]{:S(2)}) async-start(bf16[16,2,8384]{2,1,0:T(2,128)(2,1)} %reshape.284), calls=%async_computation.1 | async-start | bytes 1081344 | tf_op jit(solution)/shard_map/all_to_all | solution.py:89
  84.1 0.0 copy-done.7
  84.1 0.0 collective-permute-done
  84.1 1.1 %add_add_fusion = f32[128,1024]{1,0:T(8,128)S(1)} fusion(f32[128,1024]{1,0:T(8,128)} %collective-permute-done, f32[128,2048]{1,0:T(8,128)S(1)} %fusion.57, s32[]{:T(128)S(6)} %select_n.51, f32[1024]{0:T(1024)S(1)} %convert_element_type.64), kind=kLoop, calls=%fused_computation.42 | loop fusion | flops 262144 | bytes 1576964 | tf_op jit(solution)/shard_map/add | solution.py:94
  85.2 0.2 reshape.257
  85.5 0.7 slice.85
  86.2 0.2 fusion.53
  86.4 0.4 subtract_convert_fusion
  86.8 0.8 fusion.56
  87.6 11.3 %all-to-all-done.1 = bf16[16,2,8384]{2,1,0:T(2,128)(2,1)} async-done(((bf16[16,2,8384]{2,1,0:T(2,128)(2,1)}), bf16[16,2,8384]{2,1,0:T(2,128)(2,1)}, u32[]{:S(2)}, u32[]{:S(2)}) %all-to-all-start.1) | async-done | bytes 536608 | tf_op jit(solution)/shard_map/all_to_all | solution.py:89
  98.9 2.5 %reshape.285 = bf16[16,1,16768]{2,1,0:T(2,128)(2,1)S(1)} reshape(bf16[16,2,8384]{2,1,0:T(2,128)(2,1)} %all-to-all-done.1) | data formatting | bytes 1073152
  101.3 0.1 copy.92
  101.4 0.1 convert_bitcast_fusion
  101.5 0.1 reshape.264
  101.7 0.3 fusion.34
  101.9 0.1 fusion.52
  102.0 0.2 copy.75
  102.2 0.0 copy-start.1
  102.2 0.0 copy-done.4
  102.2 2.3 %fusion.17 = bf16[4,32,4,8,128]{4,3,0,2,1:T(8,128)(2,1)S(1)} fusion(f32[16,4,32,128]{3,2,1,0:T(8,128)S(1)} %bitcast.97, f32[16,4,32,128]{3,2,1,0:T(8,128)} %fusion.6, f32[32,4,32]{2,1,0:T(4,128)S(1)} %get-tuple-element.12, f32[32,4,32,4]{2,3,1,0:T(4,128)S(1)} %get-tuple-element.23, bf16[4,32,4,128]{3,2,1,0:T(4,128)(2,1)S(1)} %copy-done.4, ...), kind=kOutput, calls=%fused_computation.23 | convolution fusion | flops 6340608 | bytes 3391488 | tf_op jit(solution)/shard_map/bknt,tbkd->bknd/dot_general | solution.py:117
  104.5 0.2 copy.61
  104.7 1.3 %reshape.260 = bf16[4,1,32,4096]{3,2,1,0:T(8,128)(2,1)} reshape(bf16[4,32,4,8,128]{4,3,2,1,0:T(8,128)(2,1)S(1)} %copy.61) | data formatting | bytes 2097152 | tf_op jit(solution)/shard_map/reshape | solution.py:122
  (20 shorter events, 0.2 us)
Async XLA Ops:
  0.0 1.2 %copy-start = (bf16[4,1,32,4096]{3,2,1,0:T(8,128)(2,1)S(1)}, bf16[4,1,32,4096]{3,2,1,0:T(8,128)(2,1)}, u32[]{:S(2)}) copy-start(bf16[4,1,32,4096]{3,2,1,0:T(8,128)(2,1)} %param.11) | copy-start | bytes 3145732
  1.2 12.1 %copy-start.3 = (bf16[4,1,32,4096]{3,2,1,0:T(8,128)(2,1)S(1)}, bf16[4,1,32,4096]{3,2,1,0:T(8,128)(2,1)}, u32[]{:S(2)}) copy-start(bf16[4,1,32,4096]{3,2,1,0:T(8,128)(2,1)} %param.12) | copy-start | bytes 3145732
  9.4 11.3 %copy-start.5 = (s32[16,16]{1,0:T(8,128)S(1)}, s32[16,16]{1,0:T(8,128)}, u32[]{:S(2)}) copy-start(s32[16,16]{1,0:T(8,128)} %param.16) | copy-start | bytes 3076
  9.4 11.3 %copy-start.6 = (s32[16,16]{1,0:T(8,128)S(1)}, s32[16,16]{1,0:T(8,128)}, u32[]{:S(2)}) copy-start(s32[16,16]{1,0:T(8,128)} %param.17) | copy-start | bytes 3076
  9.4 12.7 %copy-start.8 = (s32[1,16]{1,0:T(1,128)S(1)}, s32[1,16]{1,0:T(1,128)}, u32[]{:S(2)}) copy-start(s32[1,16]{1,0:T(1,128)} %param.14) | copy-start | bytes 196
  10.3 73.8 %collective-permute-start = (f32[128,1024]{1,0:T(8,128)}, f32[128,1024]{1,0:T(8,128)}, u32[]{:S(2)}, u32[]{:S(2)}) collective-permute-start(f32[128,1024]{1,0:T(8,128)} %constant_dynamic-slice_fusion), channel_id=1, source_target_pairs={{0,1},{1,0},{2,3},{3,2},{4,5},{5,4},{6,7},{7,6},{8,9},{9,8},{10,11... | collective-permute-start | bytes 1572872 | tf_op jit(solution)/shard_map/ppermute | solution.py:71
  14.7 41.8 %all-to-all-start = ((bf16[16,4,32,128]{3,2,1,0:T(8,128)(2,1)}), bf16[16,4,32,128]{3,2,1,0:T(8,128)(2,1)}, u32[]{:S(2)}, u32[]{:S(2)}) async-start(bf16[16,4,32,128]{3,2,1,0:T(8,128)(2,1)} %slice_bitcast_fusion), calls=%async_computation | async-start | bytes 1048576 | tf_op jit(solution)/shard_map/all_to_all | solution.py:63
  50.5 3.8 %copy-start.2 = (bf16[1,16,128,1024]{2,3,1,0:T(8,128)(2,1)S(1)}, bf16[1,16,128,1024]{2,3,1,0:T(8,128)(2,1)}, u32[]{:S(2)}) copy-start(bf16[1,16,128,1024]{2,3,1,0:T(8,128)(2,1)} %copy.48) | copy-start | bytes 12582916
  72.5 11.6 %copy-start.7 = (bf16[1024]{0:T(1024)(128)(2,1)S(1)}, bf16[1024]{0:T(1024)(128)(2,1)}, u32[]{:S(2)}) copy-start(bf16[1024]{0:T(1024)(128)(2,1)} %param.10) | copy-start | bytes 6148
  78.1 20.8 %all-to-all-start.1 = ((bf16[16,2,8384]{2,1,0:T(2,128)(2,1)}), bf16[16,2,8384]{2,1,0:T(2,128)(2,1)}, u32[]{:S(2)}, u32[]{:S(2)}) async-start(bf16[16,2,8384]{2,1,0:T(2,128)(2,1)} %reshape.284), calls=%async_computation.1 | async-start | bytes 1081344 | tf_op jit(solution)/shard_map/all_to_all | solution.py:89
  87.6 14.6 %copy-start.4 = (bf16[4,32,4,128]{3,2,1,0:T(4,128)(2,1)S(1)}, bf16[4,32,4,128]{3,2,1,0:T(4,128)(2,1)}, u32[]{:S(2)}) copy-start(bf16[4,32,4,128]{3,2,1,0:T(4,128)(2,1)} %slice.85) | copy-start | bytes 393220
  102.2 3.8 %copy-start.1 = (bf16[4,1,32,4096]{3,2,1,0:T(8,128)(2,1)S(1)}, bf16[4,1,32,4096]{3,2,1,0:T(8,128)(2,1)}, u32[]{:S(2)}) copy-start(bf16[4,1,32,4096]{3,2,1,0:T(8,128)(2,1)} %param.11) | copy-start | bytes 3145732

commit v2 on v0

v2 whole, which is shorter than its diff:
```python
import functools
import math

import jax
import jax.numpy as jnp
from jax import lax
from jax.experimental import pallas as pl
from jax.experimental.pallas import tpu as pltpu
from jax.sharding import PartitionSpec as P

HS = 128
ROPE_BASE = 1000000.0
masked_score = -1e30
SCALE = HS ** (-0.5)
LOG2E = math.log2(math.e)
STAT = 16
GROUP = 4
MIB = 1 << 20
FULL = 60 * MIB


def each_variant(used, variants, run):
    if variants == 1:
        run(1)
        return
    for v in range(1, variants + 1):
        pl.when(used == v)(functools.partial(run, v))


def cache_copy(cache_ref, buf, sems, m, rows):
    part = pl.ds(0, rows)
    return pltpu.make_async_copy(cache_ref.at[m, part], buf.at[m, part], sems.at[m])


def moving_kernel(
    dest_ref, length_ref, query_ref, cache_ref, out_ref, buf, stats, order, sems, *, kv_heads
):
    count, capacity, _ = cache_ref.shape
    me = lax.axis_index("grp")
    chunk = min(capacity, 128)
    variants = capacity // chunk
    used = [(length_ref[me, m] + chunk - 1) // chunk for m in range(count)]
    place = [jnp.int32(0)] * (variants + 2)
    for v in range(variants, 0, -1):
        place[v - 1] = place[v] + sum((u == v).astype(jnp.int32) for u in used)
    for v in range(variants + 1):
        order[count + v] = place[v]
    for m in range(count):
        at = order[count + used[m]]
        order[count + used[m]] = at + 1
        order[at] = m
    old_body(
        lambda m: dest_ref[me, m],
        lambda i: order[i],
        lambda m: length_ref[me, m],
        lambda slot, begin, end: query_ref[slot, begin:end, :],
        cache_ref, out_ref, buf, stats, sems, kv_heads,
    )


def staying_kernel(len_ref, query_ref, cache_ref, out_ref, buf, stats, turned, sems, *, kv_heads):
    count, rows = out_ref.shape[0], out_ref.shape[1] - STAT

    def query_of(m, begin, end):
        at = pl.ds(pl.multiple_of(m * rows + begin, 8), end - begin)
        return turned[at, :].astype(jnp.bfloat16)

    def same(m):
        return m

    by_request(query_ref, turned, kv_heads, 0, count)
    old_body(
        same, same, lambda m: len_ref[m], query_of, cache_ref, out_ref, buf, stats, sems, kv_heads
    )


def old_body(
    slot_of, member, length_of, query_of, cache_ref, out_ref, buf, stats, sems, kv_heads
):
    count, capacity, _ = cache_ref.shape
    rows = out_ref.shape[1] - STAT
    per = rows // kv_heads
    chunk = min(capacity, 128)
    variants = capacity // chunk
    pair = 2 if kv_heads % 2 == 0 else 1
    def group_chunks(g):
        if variants == 1:
            return 1
        return (length_of(member(g * GROUP)) + chunk - 1) // chunk

    @pl.loop(0, count // GROUP)
    def _(g):
        def start(v):
            for i in range(GROUP):
                cache_copy(cache_ref, buf, sems, member(g * GROUP + i), v * chunk).start()

        each_variant(group_chunks(g), variants, start)

    stats[...] = jnp.zeros_like(stats)
    lane = lax.broadcasted_iota(jnp.int32, (rows, HS), 1)

    def body(g, v):
        length = v * chunk
        members = [member(g * GROUP + i) for i in range(GROUP)]
        for m in members:
            cache_copy(cache_ref, buf, sems, m, length).wait()
        slots = [slot_of(m) for m in members]
        column = lax.broadcasted_iota(jnp.int32, (pair * per, length), 1)
        part = pl.ds(0, length)
        items = [
            (i, [p * pair + j for j in range(pair)])
            for i in range(GROUP)
            for p in range(kv_heads // pair)
        ]
        queries = []
        for i, heads in items:
            own = [query_of(slots[i], h * per, (h + 1) * per) for h in heads]
            if pair == 2:
                zero = jnp.zeros_like(own[0])
                own = [
                    jnp.concatenate(
                        [jnp.concatenate([own[0], zero], 1), jnp.concatenate([zero, own[1]], 1)], 0
                    )
                ]
            queries.append(own[0])

        def columns(i, heads, shift):
            at = [h * 2 * HS + shift for h in heads]
            return jnp.concatenate([buf[members[i], part, c : c + HS] for c in at], 1)

        scores = [
            lax.dot_general(
                query, columns(i, heads, 0), (((1,), (1,)), ((), ())),
                preferred_element_type=jnp.float32,
            )
            for query, (i, heads) in zip(queries, items)
        ]
        scores = [
            jnp.where(column < length_of(members[i]), x, masked_score)
            for x, (i, _) in zip(scores, items)
        ]
        highest = [jnp.max(x, axis=1, keepdims=True) for x in scores]
        probs = [jnp.exp2((x - h) * (SCALE * LOG2E)) for x, h in zip(scores, highest)]
        total = [jnp.sum(x, axis=1, keepdims=True) for x in probs]
        probs = [x.astype(jnp.bfloat16) for x in probs]
        mixed = [
            jnp.dot(x, columns(i, heads, HS), preferred_element_type=jnp.float32)
            for x, (i, heads) in zip(probs, items)
        ]
        mixed = [x * (1.0 / t) for x, t in zip(mixed, total)]
        lses = [h * SCALE + jnp.log(t) for h, t in zip(highest, total)]
        for x, (i, heads) in zip(mixed, items):
            for j, h in enumerate(heads):
                out_ref[slots[i], h * per : (h + 1) * per, :] = x[
                    j * per : (j + 1) * per, j * HS : (j + 1) * HS
                ].astype(jnp.bfloat16)
        table = stats[0:rows, :]
        for i in range(GROUP):
            lse = jnp.concatenate([x for x, (o, _) in zip(lses, items) if o == i], 0)
            table = jnp.where(lane == slots[i], lse, table)
        stats[0:rows, :] = table

    @pl.loop(0, count // GROUP)
    def _(g):
        each_variant(group_chunks(g), variants, functools.partial(body, g))

    turned = stats[...].T
    row = lax.broadcasted_iota(jnp.int32, (STAT, HS), 0)
    for d in range(count):
        whole = jnp.broadcast_to(turned[d : d + 1, :], (STAT, HS))
        high = whole.astype(jnp.bfloat16).astype(jnp.float32)
        rest = whole - high
        middle = rest.astype(jnp.bfloat16).astype(jnp.float32)
        low = rest - middle
        terms = jnp.where(row == 0, high, jnp.where(row == 1, middle, jnp.where(row == 2, low, 0.0)))
        out_ref[d, rows : rows + STAT, :] = terms.astype(jnp.bfloat16)


def by_request(query_ref, scratch, kv_heads, first, count):
    steps, _, _, cols = query_ref.shape
    per_kv = cols // HS // kv_heads
    rows = steps * cols // HS
    for k in range(kv_heads):
        for s in range(steps):
            for q in range(per_kv):
                h = k * per_kv + q
                tile = query_ref[s, 0, first : first + count, h * HS : (h + 1) * HS].astype(jnp.float32)
                scratch[pl.ds((k * steps + s) * per_kv + q, count, stride=rows), :] = tile


def turn_kernel(query_ref, out_ref, arrived, scratch, turned, in_sems, out_sems, *, kv_heads, first):
    count, rows, _ = out_ref.shape
    per = rows // kv_heads
    width = query_ref.shape[3] // kv_heads
    own = pl.ds(first, count)

    def into(k):
        lanes = pl.ds(k * width, width)
        return pltpu.make_async_copy(
            query_ref.at[:, :, own, lanes], arrived.at[k], in_sems.at[k]
        )

    def outof(k):
        return pltpu.make_async_copy(
            turned.at[k], out_ref.at[:, pl.ds(k * per, per), :], out_sems.at[k]
        )

    for k in range(kv_heads):
        into(k).start()
    for k in range(kv_heads):
        into(k).wait()
        by_request(arrived.at[k], scratch, 1, 0, count)
        turned[k] = scratch[...].astype(jnp.bfloat16).reshape(count, per, HS)
        outof(k).start()
    for k in range(kv_heads):
        outof(k).wait()


def turn(queries, first, kv_heads):
    steps, _, serve, cols = queries.shape
    count, width = serve - first, cols // kv_heads
    per = steps * width // HS
    return pl.pallas_call(
        functools.partial(turn_kernel, kv_heads=kv_heads, first=first),
        out_shape=jax.ShapeDtypeStruct((count, kv_heads * per, HS), jnp.bfloat16),
        in_specs=[pl.BlockSpec(memory_space=pltpu.HBM)],
        out_specs=pl.BlockSpec(memory_space=pltpu.HBM),
        scratch_shapes=[
            pltpu.VMEM((kv_heads, steps, 1, count, width), jnp.bfloat16),
            pltpu.VMEM((count * per, HS), jnp.float32),
            pltpu.VMEM((kv_heads, count, per, HS), jnp.bfloat16),
            pltpu.SemaphoreType.DMA((kv_heads,)),
            pltpu.SemaphoreType.DMA((kv_heads,)),
        ],
        compiler_params=pltpu.CompilerParams(vmem_limit_bytes=FULL),
        cost_estimate=pl.CostEstimate(flops=MIB, bytes_accessed=MIB, transcendentals=0),
        name="turn",
    )(queries)


def project_kernel(index_ref, hidden_ref, weight_ref, out_ref):
    del index_ref
    out_ref[0] = jnp.dot(hidden_ref[...], weight_ref[...], preferred_element_type=jnp.float32)


def project(hidden, weight, kv_cols, tp_size, tp_index, first, pieces):
    rows, depth = hidden.shape
    width = min(kv_cols, 256)
    blocks = kv_cols // width
    return pl.pallas_call(
        project_kernel,
        out_shape=jax.ShapeDtypeStruct((pieces, rows, kv_cols), jnp.float32),
        grid_spec=pltpu.PrefetchScalarGridSpec(
            num_scalar_prefetch=1,
            grid=(pieces, blocks),
            in_specs=[
                pl.BlockSpec((rows, depth), lambda j, c, index: (0, 0)),
                pl.BlockSpec(
                    (depth, width),
                    lambda j, c, index: (0, lax.rem(index[0] + first + j, tp_size) * blocks + c),
                ),
            ],
            out_specs=pl.BlockSpec((1, rows, width), lambda j, c, index: (j, 0, c)),
        ),
        compiler_params=pltpu.CompilerParams(vmem_limit_bytes=FULL),
        cost_estimate=pl.CostEstimate(
            flops=2 * rows * depth * kv_cols * pieces,
            bytes_accessed=depth * kv_cols * pieces * 2,
            transcendentals=0,
        ),
        name="project",
    )(tp_index.reshape(1), hidden, weight)


def old_call(kernel, scalars, query, cache, rows, scratch, limit, name):
    count, capacity, _ = cache.shape
    smem, vmem = pl.BlockSpec(memory_space=pltpu.SMEM), pl.BlockSpec(memory_space=pltpu.VMEM)
    return pl.pallas_call(
        kernel,
        out_shape=jax.ShapeDtypeStruct((count, rows + STAT, HS), jnp.bfloat16),
        in_specs=[smem] * len(scalars) + [vmem, pl.BlockSpec(memory_space=pltpu.HBM)],
        out_specs=vmem,
        scratch_shapes=[
            pltpu.VMEM(cache.shape, jnp.bfloat16),
            pltpu.VMEM((128, HS), jnp.float32),
            scratch,
            pltpu.SemaphoreType.DMA((count,)),
        ],
        compiler_params=pltpu.CompilerParams(vmem_limit_bytes=limit),
        cost_estimate=pl.CostEstimate(
            flops=count * rows * capacity * HS * 8,
            bytes_accessed=cache.size * 2,
            transcendentals=count * rows * capacity,
        ),
        name=name,
    )(*scalars, query, cache)


def old_lse(stat):
    return stat[:, 0, :] + stat[:, 1, :] + stat[:, 2, :]


def merge_tiles(old, share, new_of, put, steps, per_kv, kv_heads, count, heads):
    rows = kv_heads * steps * per_kv
    for k in heads:
        for s in range(steps):
            for q in range(per_kv):
                c = (k * steps + s) * per_kv + q
                before = old[pl.ds(c, count, stride=rows), :]
                new = new_of(s, k * per_kv + q)
                put(s, k * per_kv + q, new + share[:, c : c + 1] * (before - new))


def new_kernel(
    query_ref, mine_ref, other_ref, bias_ref, cos_ref, sin_ref, old_ref, out_ref, lse_ref, scratch,
    *, kv_heads, per_kv, staying,
):
    steps, _, serve, _ = query_ref.shape
    rows = old_ref.shape[1] - STAT
    scratch[...] = old_ref[:, 0:rows, :].astype(jnp.float32).reshape(staying * rows, HS)
    raw = mine_ref[...]
    for i in range(other_ref.shape[0]):
        raw = raw + other_ref[i]
    raw = raw + bias_ref[...].astype(jnp.float32)
    total_rows = steps * serve
    request = lax.broadcasted_iota(jnp.int32, (serve, total_rows), 0)
    column = lax.broadcasted_iota(jnp.int32, (serve, total_rows), 1)
    lane = lax.broadcasted_iota(jnp.int32, (serve, HS), 1)
    lse_all = jnp.zeros((serve, HS), jnp.float32)
    for k in range(kv_heads):
        keys = raw[:, k * 2 * HS : k * 2 * HS + HS]
        keys = keys * cos_ref[...] + pltpu.roll(keys, HS // 2, 1) * sin_ref[...]
        keys = keys.astype(jnp.bfloat16)
        values = raw[:, k * 2 * HS + HS : (k + 1) * 2 * HS].astype(jnp.bfloat16)
        for s in range(steps):
            heads = [k * per_kv + q for q in range(per_kv)]
            query = jnp.concatenate([query_ref[s, 0, :, h * HS : (h + 1) * HS] for h in heads], 0)
            scores = lax.dot_general(
                query, keys, (((1,), (1,)), ((), ())), preferred_element_type=jnp.float32
            )
            seen = column == request
            for t in range(1, s + 1):
                seen = seen | (column == request + t * serve)
            scores = jnp.where(jnp.concatenate([seen] * per_kv, 0), scores, masked_score)
            highest = jnp.max(scores, axis=1, keepdims=True)
            probs = jnp.exp2((scores - highest) * (SCALE * LOG2E))
            total = jnp.sum(probs, axis=1, keepdims=True)
            mixed = jnp.dot(probs.astype(jnp.bfloat16), values, preferred_element_type=jnp.float32)
            mixed = mixed * (1.0 / total)
            lse = highest * SCALE + jnp.log(total)
            for q, h in enumerate(heads):
                c = (k * steps + s) * per_kv + q
                lse_all = jnp.where(lane == c, lse[q * serve : (q + 1) * serve], lse_all)
                out_ref[s, 0, :, h * HS : (h + 1) * HS] = mixed[
                    q * serve : (q + 1) * serve
                ].astype(jnp.bfloat16)
    lse_ref[...] = lse_all

    def put(s, h, value):
        out_ref[s, 0, 0:staying, h * HS : (h + 1) * HS] = value.astype(jnp.bfloat16)

    def new_of(s, h):
        return out_ref[s, 0, 0:staying, h * HS : (h + 1) * HS].astype(jnp.float32)

    stat = old_lse(old_ref[:, rows : rows + STAT, :].astype(jnp.float32))
    share = 1.0 / (1.0 + jnp.exp(lse_all[0:staying] - stat))
    merge_tiles(
        scratch, share, new_of, put, steps, per_kv, kv_heads, staying, range(kv_heads)
    )


def join_kernel(old_ref, new_ref, lse_ref, out_ref, arrived, scratch, merged, in_sem, out_sems, *, kv_heads, first):
    steps = new_ref.shape[0]
    count, rows = old_ref.shape[0], old_ref.shape[1] - STAT
    width = new_ref.shape[3] // kv_heads
    own = pl.ds(first, count)
    into = pltpu.make_async_copy(new_ref.at[:, :, own], arrived, in_sem)

    def outof(k):
        lanes = pl.ds(k * width, width)
        return pltpu.make_async_copy(
            merged.at[:, :, :, lanes], out_ref.at[:, :, own, lanes], out_sems.at[k]
        )

    into.start()
    scratch[...] = old_ref[:, 0:rows, :].astype(jnp.float32).reshape(count * rows, HS)
    stat = old_lse(old_ref[:, rows : rows + STAT, :].astype(jnp.float32))
    share = 1.0 / (1.0 + jnp.exp(lse_ref[first : first + count, :] - stat))
    into.wait()

    def put(s, h, value):
        merged[s, 0, :, h * HS : (h + 1) * HS] = value.astype(jnp.bfloat16)

    def new_of(s, h):
        return arrived[s, 0, :, h * HS : (h + 1) * HS].astype(jnp.float32)

    for k in range(kv_heads):
        merge_tiles(scratch, share, new_of, put, steps, width // HS, kv_heads, count, [k])
        outof(k).start()
    for k in range(kv_heads):
        outof(k).wait()


def per_device(
    kv_weight, kv_bias, hidden_in, queries, res_cache, res_len, long_cache, long_len, long_dest
):
    step_count, _, serve_rows, width_part = hidden_in.shape
    kv_cols = kv_bias.shape[0]
    kv_heads = kv_cols // (2 * HS)
    query_cols = queries.shape[3]
    head_count = query_cols // HS
    per_kv = head_count // kv_heads
    staying = res_cache.shape[1]
    moving = serve_rows - staying
    rows = head_count * step_count
    tp_size = lax.axis_size("tp")
    tp_index = lax.axis_index("tp")
    group_index = lax.axis_index("grp")
    asked = lax.all_to_all(
        turn(queries, staying, kv_heads), "grp", split_axis=0, concat_axis=0, tiled=True
    )

    flat_hidden = hidden_in.reshape(step_count * serve_rows, width_part)
    pieces = project(flat_hidden, kv_weight, kv_cols, tp_size, tp_index, 1, tp_size - 1)
    others = jnp.stack(
        [
            lax.ppermute(pieces[j], "tp", [(i, (i + j + 1) % tp_size) for i in range(tp_size)])
            for j in range(tp_size - 1)
        ]
    )
    mine = project(flat_hidden, kv_weight, kv_cols, tp_size, tp_index, 0, 1)[0]

    answer = old_call(
        functools.partial(moving_kernel, kv_heads=kv_heads),
        [long_dest, long_len],
        asked,
        long_cache[0],
        rows,
        pltpu.SMEM((moving + 8,), jnp.int32),
        48 * MIB,
        "moving_old",
    )
    answer, others, mine = lax.optimization_barrier((answer, others, mine))
    answer = lax.all_to_all(answer, "grp", split_axis=0, concat_axis=0, tiled=True)

    own_len = res_len[0]
    stayed = old_call(
        functools.partial(staying_kernel, kv_heads=kv_heads),
        [own_len],
        queries,
        res_cache[0],
        rows,
        pltpu.VMEM((staying * rows, HS), jnp.float32),
        58 * MIB,
        "staying_old",
    )
    matched = (long_dest == group_index).astype(jnp.int32)
    len_in = jnp.sum(matched * long_len, axis=1)
    served_len = jnp.concatenate([own_len, len_in])
    positions = served_len[None, :] + jnp.arange(step_count, dtype=jnp.int32)[:, None]
    half = HS // 2
    freqs = jnp.power(jnp.float32(ROPE_BASE), -2.0 * jnp.arange(half, dtype=jnp.float32) / HS)
    angles = positions.reshape(-1, 1).astype(jnp.float32) * freqs
    cosine, sine = jnp.cos(angles), jnp.sin(angles)
    cosine = jnp.concatenate([cosine, cosine], 1)
    sine = jnp.concatenate([-sine, sine], 1)

    out_shape = jax.ShapeDtypeStruct((step_count, 1, serve_rows, query_cols), jnp.bfloat16)
    fresh, lse = pl.pallas_call(
        functools.partial(new_kernel, kv_heads=kv_heads, per_kv=per_kv, staying=staying),
        out_shape=(out_shape, jax.ShapeDtypeStruct((serve_rows, HS), jnp.float32)),
        in_specs=[pl.BlockSpec(memory_space=pltpu.VMEM)] * 7,
        out_specs=(pl.BlockSpec(memory_space=pltpu.VMEM),) * 2,
        scratch_shapes=[pltpu.VMEM((staying * rows, HS), jnp.float32)],
        compiler_params=pltpu.CompilerParams(vmem_limit_bytes=24 * MIB),
        cost_estimate=pl.CostEstimate(
            flops=serve_rows * rows * step_count * serve_rows * HS * 4,
            bytes_accessed=8 * MIB,
            transcendentals=serve_rows * rows * step_count * serve_rows,
        ),
        name="new_part",
    )(queries, mine, others, kv_bias.reshape(1, kv_cols), cosine, sine, stayed)

    hbm, vmem = pl.BlockSpec(memory_space=pltpu.HBM), pl.BlockSpec(memory_space=pltpu.VMEM)
    part = (step_count, 1, moving, query_cols)
    return pl.pallas_call(
        functools.partial(join_kernel, kv_heads=kv_heads, first=staying),
        out_shape=out_shape,
        in_specs=[vmem, hbm, vmem],
        out_specs=hbm,
        scratch_shapes=[
            pltpu.VMEM(part, jnp.bfloat16),
            pltpu.VMEM((moving * rows, HS), jnp.float32),
            pltpu.VMEM(part, jnp.bfloat16),
            pltpu.SemaphoreType.DMA,
            pltpu.SemaphoreType.DMA((kv_heads,)),
        ],
        input_output_aliases={1: 0},
        compiler_params=pltpu.CompilerParams(vmem_limit_bytes=32 * MIB),
        cost_estimate=pl.CostEstimate(flops=MIB, bytes_accessed=2 * MIB, transcendentals=0),
        name="join",
    )(answer, fresh, lse)


def solution(mesh):
    placed = (
        P("tp", None),
        P("tp"),
        P(None, "grp", None, "tp"),
        P(None, "grp", None, "tp"),
        P("grp", None, None, "tp"),
        P("grp", None),
        P("grp", None, None, "tp"),
        P(),
        P(),
    )
    return jax.shard_map(
        per_device,
        mesh=mesh,
        in_specs=placed,
        out_specs=P(None, "grp", None, "tp"),
        check_vma=False,
    )
```

time: 633 us -> 56.2 us (0.09)
  the two profiles are of different devices: /device:TPU:11 before, /device:TPU:0 now
where the time goes in v2:
time: 56.2 us; the launch traced here: 55.7 us
  Pallas kernels  35.7 us (64%)
  starting transfers between devices  13.9 us (25%)
  waiting for transfers between devices  4.13 us (7%)
  local copies, waits for them, and re-layouts  1.18 us (2%)
  other arithmetic  0.62 us (1%)
    pallas_call x2, Pallas kernels, old_call(): pl.pallas_call(kernel, out_shape=jax.ShapeDtypeStruct((count, rows + STAT...  15.1 us
    pallas_call x2, Pallas kernels, project(): pl.pallas_call(project_kernel, out_shape=jax.ShapeDtypeStruct((pieces, ro...  11.9 us
    all_to_all x1, starting transfers between devices, per_device(): lax.all_to_all(turn(queries, staying, kv_heads), 'grp', split_axis=0, con...  7.37 us
    all_to_all x1, starting transfers between devices, per_device(): lax.all_to_all(answer, 'grp', split_axis=0, concat_axis=0, tiled=True)  4.99 us
    pallas_call x1, Pallas kernels, per_device(): pl.pallas_call(functools.partial(new_kernel, kv_heads=kv_heads, per_kv=pe...  3.78 us
    all_to_all x1, waiting for transfers between devices, per_device(): lax.all_to_all(answer, 'grp', split_axis=0, concat_axis=0, tiled=True)  3.09 us
    pallas_call x1, Pallas kernels, turn(): pl.pallas_call(functools.partial(turn_kernel, kv_heads=kv_heads, first=fi...  2.56 us
    pallas_call x1, Pallas kernels, per_device(): pl.pallas_call(functools.partial(join_kernel, kv_heads=kv_heads, first=st...  2.44 us
  transfers between devices with their start and end apart: 3, of which 2 were waited for; matrix products, arithmetic and copies ran while one was open for 1% of the time, Pallas kernels for 55%

profile of v2, /device:TPU:0, one launch (start us, length us, event | category | flops | bytes accessed | tf_op | source)
XLA Modules:
  0.0 55.7 jit_solution(4320158417264036309)
XLA Ops:
  0.0 2.6 %turn.1 = bf16[16,128,128]{2,1,0:T(8,128)(2,1)} custom-call(bf16[4,1,32,4096]{3,2,1,0:T(8,128)(2,1)} %query_ref.5), custom_call_target="tpu_custom_call" | custom-call | flops 1048576 | bytes 1048576 | tf_op jit(solution)/shard_map/turn/pallas_call | solution.py:223
  2.6 7.4 %all-to-all-start = ((bf16[16,128,128]{2,1,0:T(8,128)(2,1)}), bf16[16,128,128]{2,1,0:T(8,128)(2,1)S(1)}, u32[]{:S(2)}, u32[]{:S(2)}) async-start(bf16[16,128,128]{2,1,0:T(8,128)(2,1)} %turn.1), calls=%async_computation | async-start | bytes 1048576 | tf_op jit(solution)/shard_map/all_to_all | solution.py:419
  9.9 0.0 copy-start.3
  10.0 0.0 copy-start.4
  10.0 6.0 %project.2 = f32[1,128,1024]{2,1,0:T(8,128)} custom-call(s32[1]{0:T(128)} %bitcast.1.index_ref, bf16[128,4096]{1,0:T(8,128)(2,1)} %bitcast.12, bf16[4096,2048]{1,0:T(8,128)(2,1)} %weight_ref.3), custom_call_target="tpu_custom_call" | custom-call | flops 1073741824 | bytes 8388608 | tf_op jit(solution)/shard_map/project/pallas_call | solution.py:250
  15.9 0.0 copy-start.6
  15.9 0.0 copy-start.5
  15.9 1.5 %collective-permute-start = (f32[128,1024]{1,0:T(8,128)}, f32[128,1024]{1,0:T(8,128)S(1)}, u32[]{:S(2)}, u32[]{:S(2)}) collective-permute-start(f32[128,1024]{1,0:T(8,128)} %bitcast.14), channel_id=1, source_target_pairs={{0,1},{1,0},{2,3},{3,2},{4,5},{5,4},{6,7},{7,6},{8,9},{9,8},{10,11... | collective-permute-start | bytes 1572872 | tf_op jit(solution)/shard_map/ppermute | solution.py:427
  17.4 5.9 %project.3 = f32[1,128,1024]{2,1,0:T(8,128)} custom-call(s32[1]{0:T(128)} %bitcast.1.index_ref, bf16[128,4096]{1,0:T(8,128)(2,1)} %bitcast.13, bf16[4096,2048]{1,0:T(8,128)(2,1)} %weight_ref.3), custom_call_target="tpu_custom_call" | custom-call | flops 1073741824 | bytes 8388608 | tf_op jit(solution)/shard_map/project/pallas_call | solution.py:250
  23.4 0.0 copy-start
  23.4 0.0 copy-start.2
  23.4 1.0 %all-to-all-done.query_ref = bf16[16,128,128]{2,1,0:T(8,128)(2,1)S(1)} async-done(((bf16[16,128,128]{2,1,0:T(8,128)(2,1)}), bf16[16,128,128]{2,1,0:T(8,128)(2,1)S(1)}, u32[]{:S(2)}, u32[]{:S(2)}) %all-to-all-start) | async-done | bytes 524320 | tf_op jit(solution)/shard_map/all_to_all | solution.py:419
  24.4 0.0 copy-done.3
  24.4 0.0 copy-done.4
  24.4 8.2 %moving_old.1 = bf16[16,144,128]{2,1,0:T(8,128)(2,1)} custom-call(s32[16,16]{1,0:T(8,128)S(1)} %copy-done.3, s32[16,16]{1,0:T(8,128)S(1)} %copy-done.4, bf16[16,128,128]{2,1,0:T(8,128)(2,1)S(1)} %all-to-all-done.query_ref, bf16[16,512,1024]{2,1,0:T(8,128)(2,1)} %bitcast.10), custom_call_target="tpu_custom_call" | custom-call | flops 1073741824 | bytes 16777216 | tf_op jit(solution)/shard_map/moving_old/pallas_call | solution.py:278
  32.7 0.0 collective-permute-done
  32.7 5.0 %all-to-all-start.1 = ((bf16[16,144,128]{2,1,0:T(8,128)(2,1)}), bf16[16,144,128]{2,1,0:T(8,128)(2,1)S(1)}, u32[]{:S(2)}, u32[]{:S(2)}) async-start(bf16[16,144,128]{2,1,0:T(8,128)(2,1)} %moving_old.1), calls=%async_computation.1 | async-start | bytes 1179648 | tf_op jit(solution)/shard_map/all_to_all | solution.py:444
  37.7 0.1 select_reduce_fusion
  37.8 0.0 copy-done.6
  37.8 0.1 pad_add_fusion
  37.9 0.1 convert_element_type.13
  38.0 0.0 copy-done.5
  38.0 6.8 %staying_old.1.old_ref = bf16[16,144,128]{2,1,0:T(8,128)(2,1)} custom-call(s32[16]{0:T(128)} %bitcast.15, bf16[4,1,32,4096]{3,2,1,0:T(8,128)(2,1)} %query_ref.5, bf16[16,128,1024]{2,1,0:T(8,128)(2,1)} %bitcast.11), custom_call_target="tpu_custom_call" | custom-call | flops 268435456 | bytes 4194304 | tf_op jit(solution)/shard_map/staying_old/pallas_call | solution.py:278
  44.8 0.3 fusion
  45.2 0.1 pad_maximum_fusion
  45.3 0.0 copy-done
  45.3 0.0 copy-done.2
  45.3 0.0 copy-start.1
  45.3 1.1 %copy-done.1 = bf16[16,144,128]{2,1,0:T(8,128)(2,1)S(1)} copy-done((bf16[16,144,128]{2,1,0:T(8,128)(2,1)S(1)}, bf16[16,144,128]{2,1,0:T(8,128)(2,1)}, u32[]{:S(2)}) %copy-start.1) | copy-done | bytes 589848
  46.3 3.8 %new_part.1 = (bf16[4,1,32,4096]{3,2,1,0:T(8,128)(2,1)}, f32[32,128]{1,0:T(8,128)S(1)}) custom-call(bf16[4,1,32,4096]{3,2,1,0:T(8,128)(2,1)S(1)} %copy-done, f32[128,1024]{1,0:T(8,128)S(1)} %bitcast.8, f32[1,128,1024]{2,1,0:T(8,128)S(1)} %bitcast.9, bf16[1,1024]{1,0:T(2,128)(2,1)S(1)} %reshape.35.bias_ref, f32[128,128]{1,0:T(8,128)S(1)} %get-tuple-element.18.cos_ref, ...), custom_call_target="tpu_custom_call" | custom-call | flops 268435456 | bytes 8388608 | tf_op jit(solution)/shard_map/new_part/pallas_call | solution.py:469
  50.1 3.1 %all-to-all-done.1.old_ref = bf16[16,144,128]{2,1,0:T(8,128)(2,1)S(1)} async-done(((bf16[16,144,128]{2,1,0:T(8,128)(2,1)}), bf16[16,144,128]{2,1,0:T(8,128)(2,1)S(1)}, u32[]{:S(2)}, u32[]{:S(2)}) %all-to-all-start.1) | async-done | bytes 589856 | tf_op jit(solution)/shard_map/all_to_all | solution.py:444
  53.2 2.4 %join.1 = bf16[4,1,32,4096]{3,2,1,0:T(8,128)(2,1)} custom-call(bf16[16,144,128]{2,1,0:T(8,128)(2,1)S(1)} %all-to-all-done.1.old_ref, bf16[4,1,32,4096]{3,2,1,0:T(8,128)(2,1)} %get-tuple-element.13.new_ref, f32[32,128]{1,0:T(8,128)S(1)} %get-tuple-element.14.lse_ref), custom_call_target="tpu_custom_call", output_to_operand_aliasing={{}: (1, {})} | custom-call | flops 1048576 | bytes 2097152 | tf_op jit(solution)/shard_map/join/pallas_call | solution.py:486
  (3 shorter events, 0.0 us)
Async XLA Ops:
  2.6 21.8 %all-to-all-start = ((bf16[16,128,128]{2,1,0:T(8,128)(2,1)}), bf16[16,128,128]{2,1,0:T(8,128)(2,1)S(1)}, u32[]{:S(2)}, u32[]{:S(2)}) async-start(bf16[16,128,128]{2,1,0:T(8,128)(2,1)} %turn.1), calls=%async_computation | async-start | bytes 1048576 | tf_op jit(solution)/shard_map/all_to_all | solution.py:419
  9.9 14.5 %copy-start.3 = (s32[16,16]{1,0:T(8,128)S(1)}, s32[16,16]{1,0:T(8,128)}, u32[]{:S(2)}) copy-start(s32[16,16]{1,0:T(8,128)} %dest_ref.1) | copy-start | bytes 3076
  10.0 14.5 %copy-start.4 = (s32[16,16]{1,0:T(8,128)S(1)}, s32[16,16]{1,0:T(8,128)}, u32[]{:S(2)}) copy-start(s32[16,16]{1,0:T(8,128)} %length_ref.1) | copy-start | bytes 3076
  15.9 21.9 %copy-start.6 = (s32[1,16]{1,0:T(1,128)S(1)}, s32[1,16]{1,0:T(1,128)}, u32[]{:S(2)}) copy-start(s32[1,16]{1,0:T(1,128)} %param.14) | copy-start | bytes 196
  15.9 22.0 %copy-start.5 = (bf16[1024]{0:T(1024)(128)(2,1)S(1)}, bf16[1024]{0:T(1024)(128)(2,1)}, u32[]{:S(2)}) copy-start(bf16[1024]{0:T(1024)(128)(2,1)} %param.10) | copy-start | bytes 6148
  15.9 16.7 %collective-permute-start = (f32[128,1024]{1,0:T(8,128)}, f32[128,1024]{1,0:T(8,128)S(1)}, u32[]{:S(2)}, u32[]{:S(2)}) collective-permute-start(f32[128,1024]{1,0:T(8,128)} %bitcast.14), channel_id=1, source_target_pairs={{0,1},{1,0},{2,3},{3,2},{4,5},{5,4},{6,7},{7,6},{8,9},{9,8},{10,11... | collective-permute-start | bytes 1572872 | tf_op jit(solution)/shard_map/ppermute | solution.py:427
  23.4 21.9 %copy-start = (bf16[4,1,32,4096]{3,2,1,0:T(8,128)(2,1)S(1)}, bf16[4,1,32,4096]{3,2,1,0:T(8,128)(2,1)}, u32[]{:S(2)}) copy-start(bf16[4,1,32,4096]{3,2,1,0:T(8,128)(2,1)} %query_ref.5) | copy-start | bytes 3145732
  23.4 21.9 %copy-start.2 = (f32[1,128,1024]{2,1,0:T(8,128)S(1)}, f32[1,128,1024]{2,1,0:T(8,128)}, u32[]{:S(2)}) copy-start(f32[1,128,1024]{2,1,0:T(8,128)} %project.3) | copy-start | bytes 1572868
  32.7 20.6 %all-to-all-start.1 = ((bf16[16,144,128]{2,1,0:T(8,128)(2,1)}), bf16[16,144,128]{2,1,0:T(8,128)(2,1)S(1)}, u32[]{:S(2)}, u32[]{:S(2)}) async-start(bf16[16,144,128]{2,1,0:T(8,128)(2,1)} %moving_old.1), calls=%async_computation.1 | async-start | bytes 1179648 | tf_op jit(solution)/shard_map/all_to_all | solution.py:444
  45.3 1.1 %copy-start.1 = (bf16[16,144,128]{2,1,0:T(8,128)(2,1)S(1)}, bf16[16,144,128]{2,1,0:T(8,128)(2,1)}, u32[]{:S(2)}) copy-start(bf16[16,144,128]{2,1,0:T(8,128)(2,1)} %staying_old.1.old_ref) | copy-start | bytes 1769476

commit v3 on v2

--- a/solution.py
+++ b/solution.py
@@ -13,95 +13,122 @@
 masked_score = -1e30
 SCALE = HS ** (-0.5)
 LOG2E = math.log2(math.e)
-STAT = 16
+STAT = 8
 GROUP = 4
 MIB = 1 << 20
 FULL = 60 * MIB
 
 
-def each_variant(used, variants, run):
-    if variants == 1:
-        run(1)
-        return
-    for v in range(1, variants + 1):
-        pl.when(used == v)(functools.partial(run, v))
-
-
 def cache_copy(cache_ref, buf, sems, m, rows):
     part = pl.ds(0, rows)
     return pltpu.make_async_copy(cache_ref.at[m, part], buf.at[m, part], sems.at[m])
 
 
 def moving_kernel(
-    dest_ref, length_ref, query_ref, cache_ref, out_ref, buf, stats, order, sems, *, kv_heads
+    dest_ref, length_ref, query_ref, cache_ref, out_ref,
+    buf, order, answers, in_sems, out_sems, *, kv_heads,
 ):
     count, capacity, _ = cache_ref.shape
     me = lax.axis_index("grp")
     chunk = min(capacity, 128)
     variants = capacity // chunk
     used = [(length_ref[me, m] + chunk - 1) // chunk for m in range(count)]
-    place = [jnp.int32(0)] * (variants + 2)
-    for v in range(variants, 0, -1):
-        place[v - 1] = place[v] + sum((u == v).astype(jnp.int32) for u in used)
-    for v in range(variants + 1):
-        order[count + v] = place[v]
+    place = jnp.int32(0)
+    for v in range(1, variants + 1):
+        order[count + v] = place
+        place = place + sum((u == v).astype(jnp.int32) for u in used)
     for m in range(count):
         at = order[count + used[m]]
         order[count + used[m]] = at + 1
         order[at] = m
+
+    def leave(slot):
+        return pltpu.make_async_copy(answers.at[slot], out_ref.at[slot], out_sems.at[slot])
+
     old_body(
         lambda m: dest_ref[me, m],
         lambda i: order[i],
         lambda m: length_ref[me, m],
         lambda slot, begin, end: query_ref[slot, begin:end, :],
-        cache_ref, out_ref, buf, stats, sems, kv_heads,
-    )
-
-
-def staying_kernel(len_ref, query_ref, cache_ref, out_ref, buf, stats, turned, sems, *, kv_heads):
+        cache_ref, answers, buf, in_sems, kv_heads, lambda slot: leave(slot).start(),
+    )
+
+    @pl.loop(0, count)
+    def _(slot):
+        leave(slot).wait()
+
+
+def staying_kernel(len_ref, query_ref, cache_ref, out_ref, buf, turned, sems, *, kv_heads):
     count, rows = out_ref.shape[0], out_ref.shape[1] - STAT
 
-    def query_of(m, begin, end):
-        at = pl.ds(pl.multiple_of(m * rows + begin, 8), end - begin)
-        return turned[at, :].astype(jnp.bfloat16)
+    steps, per = query_ref.shape[0], rows // kv_heads
 
     def same(m):
         return m
 
-    by_request(query_ref, turned, kv_heads, 0, count)
+    for k in range(kv_heads):
+        turned[:, k * per : (k + 1) * per, :] = by_request(
+            lambda s, q: query_ref[s, 0, 0:count, pl.ds((k * per // steps + q) * HS, HS)],
+            steps, per // steps,
+        )
     old_body(
-        same, same, lambda m: len_ref[m], query_of, cache_ref, out_ref, buf, stats, sems, kv_heads
-    )
-
-
-def old_body(
-    slot_of, member, length_of, query_of, cache_ref, out_ref, buf, stats, sems, kv_heads
-):
+        same, same, lambda m: len_ref[m], lambda m, begin, end: turned[m, begin:end, :],
+        cache_ref, out_ref, buf, sems, kv_heads, lambda slot: None,
+    )
+
+
+def stat_rows(lses):
+    rows = lses[0].shape[0]
+    same = lax.broadcasted_iota(jnp.int32, (rows, HS), 0) == lax.broadcasted_iota(
+        jnp.int32, (rows, HS), 1
+    )
+    row = lax.broadcasted_iota(jnp.int32, (STAT, HS), 0)
+    result = []
+    for lse in lses:
+        turned = jnp.sum(jnp.where(same, lse, 0.0), axis=0, keepdims=True)
+        whole = jnp.broadcast_to(turned, (STAT, HS))
+        high = whole.astype(jnp.bfloat16).astype(jnp.float32)
+        rest = whole - high
+        middle = rest.astype(jnp.bfloat16).astype(jnp.float32)
+        terms = jnp.where(row == 0, high, jnp.where(row == 1, middle, rest - middle))
+        result.append(jnp.where(row < 3, terms, 0.0).astype(jnp.bfloat16))
+    return result
+
+
+def old_body(slot_of, member, length_of, query_of, cache_ref, out_ref, buf, sems, kv_heads, done):
     count, capacity, _ = cache_ref.shape
     rows = out_ref.shape[1] - STAT
     per = rows // kv_heads
     chunk = min(capacity, 128)
     variants = capacity // chunk
     pair = 2 if kv_heads % 2 == 0 else 1
-    def group_chunks(g):
-        if variants == 1:
-            return 1
-        return (length_of(member(g * GROUP)) + chunk - 1) // chunk
-
-    @pl.loop(0, count // GROUP)
-    def _(g):
-        def start(v):
-            for i in range(GROUP):
-                cache_copy(cache_ref, buf, sems, member(g * GROUP + i), v * chunk).start()
-
-        each_variant(group_chunks(g), variants, start)
-
-    stats[...] = jnp.zeros_like(stats)
-    lane = lax.broadcasted_iota(jnp.int32, (rows, HS), 1)
-
-    def body(g, v):
+    part_size = [GROUP]
+
+    def run(act):
+        def one(first, size):
+            if variants == 1:
+                act(first, size, 1)
+                return
+            used = (length_of(member(first + size - 1)) + chunk - 1) // chunk
+            for v in range(1, variants + 1):
+                pl.when(used == v)(functools.partial(act, first, size, v))
+
+        @pl.loop(0, count // GROUP - 1)
+        def _(g):
+            one(g * GROUP, GROUP)
+
+        first = count - GROUP
+        for size in part_size:
+            one(first, size)
+            first += size
+
+    def start(first, size, v):
+        for i in range(size):
+            cache_copy(cache_ref, buf, sems, member(first + i), v * chunk).start()
+
+    def body(first, size, v):
         length = v * chunk
-        members = [member(g * GROUP + i) for i in range(GROUP)]
+        members = [member(first + i) for i in range(size)]
         for m in members:
             cache_copy(cache_ref, buf, sems, m, length).wait()
         slots = [slot_of(m) for m in members]
@@ -109,7 +136,7 @@
         part = pl.ds(0, length)
         items = [
             (i, [p * pair + j for j in range(pair)])
-            for i in range(GROUP)
+            for i in range(size)
             for p in range(kv_heads // pair)
         ]
         queries = []
@@ -149,47 +176,33 @@
         ]
         mixed = [x * (1.0 / t) for x, t in zip(mixed, total)]
         lses = [h * SCALE + jnp.log(t) for h, t in zip(highest, total)]
+        terms = stat_rows(
+            [
+                jnp.concatenate([x for x, (o, _) in zip(lses, items) if o == i], 0)
+                for i in range(size)
+            ]
+        )
         for x, (i, heads) in zip(mixed, items):
             for j, h in enumerate(heads):
                 out_ref[slots[i], h * per : (h + 1) * per, :] = x[
                     j * per : (j + 1) * per, j * HS : (j + 1) * HS
                 ].astype(jnp.bfloat16)
-        table = stats[0:rows, :]
-        for i in range(GROUP):
-            lse = jnp.concatenate([x for x, (o, _) in zip(lses, items) if o == i], 0)
-            table = jnp.where(lane == slots[i], lse, table)
-        stats[0:rows, :] = table
-
-    @pl.loop(0, count // GROUP)
-    def _(g):
-        each_variant(group_chunks(g), variants, functools.partial(body, g))
-
-    turned = stats[...].T
-    row = lax.broadcasted_iota(jnp.int32, (STAT, HS), 0)
-    for d in range(count):
-        whole = jnp.broadcast_to(turned[d : d + 1, :], (STAT, HS))
-        high = whole.astype(jnp.bfloat16).astype(jnp.float32)
-        rest = whole - high
-        middle = rest.astype(jnp.bfloat16).astype(jnp.float32)
-        low = rest - middle
-        terms = jnp.where(row == 0, high, jnp.where(row == 1, middle, jnp.where(row == 2, low, 0.0)))
-        out_ref[d, rows : rows + STAT, :] = terms.astype(jnp.bfloat16)
-
-
-def by_request(query_ref, scratch, kv_heads, first, count):
-    steps, _, _, cols = query_ref.shape
-    per_kv = cols // HS // kv_heads
-    rows = steps * cols // HS
-    for k in range(kv_heads):
-        for s in range(steps):
-            for q in range(per_kv):
-                h = k * per_kv + q
-                tile = query_ref[s, 0, first : first + count, h * HS : (h + 1) * HS].astype(jnp.float32)
-                scratch[pl.ds((k * steps + s) * per_kv + q, count, stride=rows), :] = tile
-
-
-def turn_kernel(query_ref, out_ref, arrived, scratch, turned, in_sems, out_sems, *, kv_heads, first):
+        for i in range(size):
+            out_ref[slots[i], rows : rows + STAT, :] = terms[i]
+            done(slots[i])
+
+    run(start)
+    run(body)
+
+
+def by_request(tile_of, steps, per_kv):
+    tiles = [tile_of(s, q) for s in range(steps) for q in range(per_kv)]
+    return jnp.swapaxes(jnp.stack(tiles, 0), 0, 1)
+
+
+def turn_kernel(query_ref, out_ref, arrived, turned, in_sems, out_sems, *, kv_heads, first):
     count, rows, _ = out_ref.shape
+    steps = query_ref.shape[0]
     per = rows // kv_heads
     width = query_ref.shape[3] // kv_heads
     own = pl.ds(first, count)
@@ -209,8 +222,9 @@
         into(k).start()
     for k in range(kv_heads):
         into(k).wait()
-        by_request(arrived.at[k], scratch, 1, 0, count)
-        turned[k] = scratch[...].astype(jnp.bfloat16).reshape(count, per, HS)
+        turned[k] = by_request(
+            lambda s, q: arrived[k, s, 0, :, q * HS : (q + 1) * HS], steps, per // steps
+        )
         outof(k).start()
     for k in range(kv_heads):
         outof(k).wait()
@@ -227,7 +241,6 @@
         out_specs=pl.BlockSpec(memory_space=pltpu.HBM),
         scratch_shapes=[
             pltpu.VMEM((kv_heads, steps, 1, count, width), jnp.bfloat16),
-            pltpu.VMEM((count * per, HS), jnp.float32),
             pltpu.VMEM((kv_heads, count, per, HS), jnp.bfloat16),
             pltpu.SemaphoreType.DMA((kv_heads,)),
             pltpu.SemaphoreType.DMA((kv_heads,)),
@@ -272,20 +285,15 @@
     )(tp_index.reshape(1), hidden, weight)
 
 
-def old_call(kernel, scalars, query, cache, rows, scratch, limit, name):
+def old_call(kernel, scalars, query, cache, rows, scratch, out_space, limit, name):
     count, capacity, _ = cache.shape
     smem, vmem = pl.BlockSpec(memory_space=pltpu.SMEM), pl.BlockSpec(memory_space=pltpu.VMEM)
     return pl.pallas_call(
         kernel,
         out_shape=jax.ShapeDtypeStruct((count, rows + STAT, HS), jnp.bfloat16),
         in_specs=[smem] * len(scalars) + [vmem, pl.BlockSpec(memory_space=pltpu.HBM)],
-        out_specs=vmem,
-        scratch_shapes=[
-            pltpu.VMEM(cache.shape, jnp.bfloat16),
-            pltpu.VMEM((128, HS), jnp.float32),
-            scratch,
-            pltpu.SemaphoreType.DMA((count,)),
-        ],
+        out_specs=pl.BlockSpec(memory_space=out_space),
+        scratch_shapes=[pltpu.VMEM(cache.shape, jnp.bfloat16)] + scratch,
         compiler_params=pltpu.CompilerParams(vmem_limit_bytes=limit),
         cost_estimate=pl.CostEstimate(
             flops=count * rows * capacity * HS * 8,
@@ -300,24 +308,23 @@
     return stat[:, 0, :] + stat[:, 1, :] + stat[:, 2, :]
 
 
-def merge_tiles(old, share, new_of, put, steps, per_kv, kv_heads, count, heads):
-    rows = kv_heads * steps * per_kv
-    for k in heads:
-        for s in range(steps):
-            for q in range(per_kv):
-                c = (k * steps + s) * per_kv + q
-                before = old[pl.ds(c, count, stride=rows), :]
-                new = new_of(s, k * per_kv + q)
-                put(s, k * per_kv + q, new + share[:, c : c + 1] * (before - new))
+def merge_head(old_ref, share, new_of, put, steps, per_kv, k):
+    per = steps * per_kv
+    old = jnp.swapaxes(old_ref[:, k * per : (k + 1) * per, :], 0, 1).astype(jnp.float32)
+    for s in range(steps):
+        for q in range(per_kv):
+            at = s * per_kv + q
+            c = k * per + at
+            new = new_of(s, k * per_kv + q)
+            put(s, k * per_kv + q, new + share[:, c : c + 1] * (old[at] - new))
 
 
 def new_kernel(
-    query_ref, mine_ref, other_ref, bias_ref, cos_ref, sin_ref, old_ref, out_ref, lse_ref, scratch,
+    query_ref, mine_ref, other_ref, bias_ref, cos_ref, sin_ref, old_ref, out_ref, lse_ref,
     *, kv_heads, per_kv, staying,
 ):
     steps, _, serve, _ = query_ref.shape
     rows = old_ref.shape[1] - STAT
-    scratch[...] = old_ref[:, 0:rows, :].astype(jnp.float32).reshape(staying * rows, HS)
     raw = mine_ref[...]
     for i in range(other_ref.shape[0]):
         raw = raw + other_ref[i]
@@ -364,38 +371,39 @@
 
     stat = old_lse(old_ref[:, rows : rows + STAT, :].astype(jnp.float32))
     share = 1.0 / (1.0 + jnp.exp(lse_all[0:staying] - stat))
-    merge_tiles(
-        scratch, share, new_of, put, steps, per_kv, kv_heads, staying, range(kv_heads)
-    )
-
-
-def join_kernel(old_ref, new_ref, lse_ref, out_ref, arrived, scratch, merged, in_sem, out_sems, *, kv_heads, first):
+    for k in range(kv_heads):
+        merge_head(old_ref, share, new_of, put, steps, per_kv, k)
+
+
+def join_kernel(old_ref, new_ref, lse_ref, out_ref, arrived, merged, in_sems, out_sems, *, kv_heads, first):
     steps = new_ref.shape[0]
     count, rows = old_ref.shape[0], old_ref.shape[1] - STAT
     width = new_ref.shape[3] // kv_heads
     own = pl.ds(first, count)
-    into = pltpu.make_async_copy(new_ref.at[:, :, own], arrived, in_sem)
+
+    def into(k):
+        lanes = pl.ds(k * width, width)
+        return pltpu.make_async_copy(new_ref.at[:, :, own, lanes], arrived.at[k], in_sems.at[k])
 
     def outof(k):
         lanes = pl.ds(k * width, width)
-        return pltpu.make_async_copy(
-            merged.at[:, :, :, lanes], out_ref.at[:, :, own, lanes], out_sems.at[k]
-        )
-
-    into.start()
-    scratch[...] = old_ref[:, 0:rows, :].astype(jnp.float32).reshape(count * rows, HS)
+        return pltpu.make_async_copy(merged.at[k], out_ref.at[:, :, own, lanes], out_sems.at[k])
+
+    for k in range(kv_heads):
+        into(k).start()
     stat = old_lse(old_ref[:, rows : rows + STAT, :].astype(jnp.float32))
     share = 1.0 / (1.0 + jnp.exp(lse_ref[first : first + count, :] - stat))
-    into.wait()
-
-    def put(s, h, value):
-        merged[s, 0, :, h * HS : (h + 1) * HS] = value.astype(jnp.bfloat16)
-
-    def new_of(s, h):
-        return arrived[s, 0, :, h * HS : (h + 1) * HS].astype(jnp.float32)
-
-    for k in range(kv_heads):
-        merge_tiles(scratch, share, new_of, put, steps, width // HS, kv_heads, count, [k])
+    for k in range(kv_heads):
+        base = k * width
+
+        def put(s, h, value):
+            merged[k, s, 0, :, h * HS - base : (h + 1) * HS - base] = value.astype(jnp.bfloat16)
+
+        def new_of(s, h):
+            return arrived[k, s, 0, :, h * HS - base : (h + 1) * HS - base].astype(jnp.float32)
+
+        into(k).wait()
+        merge_head(old_ref, share, new_of, put, steps, width // HS, k)
         outof(k).start()
     for k in range(kv_heads):
         outof(k).wait()
@@ -436,7 +444,13 @@
         asked,
         long_cache[0],
         rows,
-        pltpu.SMEM((moving + 8,), jnp.int32),
+        [
+            pltpu.SMEM((moving + 8,), jnp.int32),
+            pltpu.VMEM((moving, rows + STAT, HS), jnp.bfloat16),
+            pltpu.SemaphoreType.DMA((moving,)),
+            pltpu.SemaphoreType.DMA((moving,)),
+        ],
+        pltpu.HBM,
         48 * MIB,
         "moving_old",
     )
@@ -450,7 +464,8 @@
         queries,
         res_cache[0],
         rows,
-        pltpu.VMEM((staying * rows, HS), jnp.float32),
+        [pltpu.VMEM((staying, rows, HS), jnp.bfloat16), pltpu.SemaphoreType.DMA((staying,))],
+        pltpu.VMEM,
         58 * MIB,
         "staying_old",
     )
@@ -471,7 +486,6 @@
         out_shape=(out_shape, jax.ShapeDtypeStruct((serve_rows, HS), jnp.float32)),
         in_specs=[pl.BlockSpec(memory_space=pltpu.VMEM)] * 7,
         out_specs=(pl.BlockSpec(memory_space=pltpu.VMEM),) * 2,
-        scratch_shapes=[pltpu.VMEM((staying * rows, HS), jnp.float32)],
         compiler_params=pltpu.CompilerParams(vmem_limit_bytes=24 * MIB),
         cost_estimate=pl.CostEstimate(
             flops=serve_rows * rows * step_count * serve_rows * HS * 4,
@@ -482,7 +496,7 @@
     )(queries, mine, others, kv_bias.reshape(1, kv_cols), cosine, sine, stayed)
 
     hbm, vmem = pl.BlockSpec(memory_space=pltpu.HBM), pl.BlockSpec(memory_space=pltpu.VMEM)
-    part = (step_count, 1, moving, query_cols)
+    part = (kv_heads, step_count, 1, moving, query_cols // kv_heads)
     return pl.pallas_call(
         functools.partial(join_kernel, kv_heads=kv_heads, first=staying),
         out_shape=out_shape,
@@ -490,9 +504,8 @@
         out_specs=hbm,
         scratch_shapes=[
             pltpu.VMEM(part, jnp.bfloat16),
-            pltpu.VMEM((moving * rows, HS), jnp.float32),
             pltpu.VMEM(part, jnp.bfloat16),
-            pltpu.SemaphoreType.DMA,
+            pltpu.SemaphoreType.DMA((kv_heads,)),
             pltpu.SemaphoreType.DMA((kv_heads,)),
         ],
         input_output_aliases={1: 0},

time: 56.2 us -> 54.4 us (0.968)
  Pallas kernels: 35.7 us -> 33.2 us
    pallas_call x2, Pallas kernels: 15.1 us -> 13.5 us  [old_call(): pl.pallas_call(kernel, out_shape=jax.ShapeDtypeStruct((count, rows + STAT...]
    pallas_call x1, Pallas kernels: 2.56 us -> 1.85 us  [turn(): pl.pallas_call(functools.partial(turn_kernel, kv_heads=kv_heads, first=fi...]
  transfers between devices with their start and end apart: 3 -> 3, of which waited for: 2 -> 2; matrix products, arithmetic and copies ran while one was open for 1% -> 1% of each run, Pallas kernels for 55% -> 54%
where the time goes in v3:
time: 54.4 us; the launch traced here: 53.9 us
  Pallas kernels  33.2 us (61%)
  starting transfers between devices  14.2 us (26%)
  waiting for transfers between devices  4.52 us (8%)
  local copies, waits for them, and re-layouts  1.17 us (2%)
  other arithmetic  0.62 us (1%)
    pallas_call x2, Pallas kernels, old_call(): pl.pallas_call(kernel, out_shape=jax.ShapeDtypeStruct((count, rows + STAT...  13.5 us
    pallas_call x2, Pallas kernels, project(): pl.pallas_call(project_kernel, out_shape=jax.ShapeDtypeStruct((pieces, ro...  11.9 us
    all_to_all x1, starting transfers between devices, per_device(): lax.all_to_all(turn(queries, staying, kv_heads), 'grp', split_axis=0, con...  7.37 us
    all_to_all x1, starting transfers between devices, per_device(): lax.all_to_all(answer, 'grp', split_axis=0, concat_axis=0, tiled=True)  5.29 us
    pallas_call x1, Pallas kernels, per_device(): pl.pallas_call(functools.partial(new_kernel, kv_heads=kv_heads, per_kv=pe...  3.61 us
    all_to_all x1, waiting for transfers between devices, per_device(): lax.all_to_all(answer, 'grp', split_axis=0, concat_axis=0, tiled=True)  3.47 us
    pallas_call x1, Pallas kernels, per_device(): pl.pallas_call(functools.partial(join_kernel, kv_heads=kv_heads, first=st...  2.33 us
    pallas_call x1, Pallas kernels, turn(): pl.pallas_call(functools.partial(turn_kernel, kv_heads=kv_heads, first=fi...  1.85 us
  transfers between devices with their start and end apart: 3, of which 2 were waited for; matrix products, arithmetic and copies ran while one was open for 1% of the time, Pallas kernels for 54%

profile of v3, /device:TPU:0, one launch (start us, length us, event | category | flops | bytes accessed | tf_op | source)
XLA Modules:
  0.0 53.9 jit_solution(12722791629754603520)
XLA Ops:
  0.0 1.9 %turn.1 = bf16[16,128,128]{2,1,0:T(8,128)(2,1)} custom-call(bf16[4,1,32,4096]{3,2,1,0:T(8,128)(2,1)} %query_ref.5), custom_call_target="tpu_custom_call" | custom-call | flops 1048576 | bytes 1048576 | tf_op jit(solution)/shard_map/turn/pallas_call | solution.py:237
  1.9 7.4 %all-to-all-start = ((bf16[16,128,128]{2,1,0:T(8,128)(2,1)}), bf16[16,128,128]{2,1,0:T(8,128)(2,1)S(1)}, u32[]{:S(2)}, u32[]{:S(2)}) async-start(bf16[16,128,128]{2,1,0:T(8,128)(2,1)} %turn.1), calls=%async_computation | async-start | bytes 1048576 | tf_op jit(solution)/shard_map/all_to_all | solution.py:427
  9.2 0.0 copy-start.3
  9.3 0.0 copy-start.4
  9.3 5.9 %project.2 = f32[1,128,1024]{2,1,0:T(8,128)} custom-call(s32[1]{0:T(128)} %bitcast.1.index_ref, bf16[128,4096]{1,0:T(8,128)(2,1)} %bitcast.12, bf16[4096,2048]{1,0:T(8,128)(2,1)} %weight_ref.3), custom_call_target="tpu_custom_call" | custom-call | flops 1073741824 | bytes 8388608 | tf_op jit(solution)/shard_map/project/pallas_call | solution.py:263
  15.2 0.0 copy-start.6
  15.2 0.0 copy-start.5
  15.2 1.5 %collective-permute-start = (f32[128,1024]{1,0:T(8,128)}, f32[128,1024]{1,0:T(8,128)S(1)}, u32[]{:S(2)}, u32[]{:S(2)}) collective-permute-start(f32[128,1024]{1,0:T(8,128)} %bitcast.14), channel_id=1, source_target_pairs={{0,1},{1,0},{2,3},{3,2},{4,5},{5,4},{6,7},{7,6},{8,9},{9,8},{10,11... | collective-permute-start | bytes 1572872 | tf_op jit(solution)/shard_map/ppermute | solution.py:435
  16.7 5.9 %project.3 = f32[1,128,1024]{2,1,0:T(8,128)} custom-call(s32[1]{0:T(128)} %bitcast.1.index_ref, bf16[128,4096]{1,0:T(8,128)(2,1)} %bitcast.13, bf16[4096,2048]{1,0:T(8,128)(2,1)} %weight_ref.3), custom_call_target="tpu_custom_call" | custom-call | flops 1073741824 | bytes 8388608 | tf_op jit(solution)/shard_map/project/pallas_call | solution.py:263
  22.7 0.0 copy-start
  22.7 0.0 copy-start.2
  22.7 1.0 %all-to-all-done.query_ref = bf16[16,128,128]{2,1,0:T(8,128)(2,1)S(1)} async-done(((bf16[16,128,128]{2,1,0:T(8,128)(2,1)}), bf16[16,128,128]{2,1,0:T(8,128)(2,1)S(1)}, u32[]{:S(2)}, u32[]{:S(2)}) %all-to-all-start) | async-done | bytes 524320 | tf_op jit(solution)/shard_map/all_to_all | solution.py:427
  23.7 0.0 copy-done.3
  23.7 0.0 copy-done.4
  23.7 7.4 %moving_old.1 = bf16[16,136,128]{2,1,0:T(8,128)(2,1)} custom-call(s32[16,16]{1,0:T(8,128)S(1)} %copy-done.3, s32[16,16]{1,0:T(8,128)S(1)} %copy-done.4, bf16[16,128,128]{2,1,0:T(8,128)(2,1)S(1)} %all-to-all-done.query_ref, bf16[16,512,1024]{2,1,0:T(8,128)(2,1)} %bitcast.10), custom_call_target="tpu_custom_call" | custom-call | flops 1073741824 | bytes 16777216 | tf_op jit(solution)/shard_map/moving_old/pallas_call | solution.py:291
  31.1 0.0 collective-permute-done
  31.1 5.3 %all-to-all-start.1 = ((bf16[16,136,128]{2,1,0:T(8,128)(2,1)}), bf16[16,136,128]{2,1,0:T(8,128)(2,1)S(1)}, u32[]{:S(2)}, u32[]{:S(2)}) async-start(bf16[16,136,128]{2,1,0:T(8,128)(2,1)} %moving_old.1), calls=%async_computation.1 | async-start | bytes 1114112 | tf_op jit(solution)/shard_map/all_to_all | solution.py:458
  36.4 0.1 select_reduce_fusion
  36.5 0.0 copy-done.6
  36.5 0.1 pad_add_fusion
  36.6 0.1 convert_element_type.13
  36.7 0.0 copy-done.5
  36.7 6.1 %staying_old.1.old_ref = bf16[16,136,128]{2,1,0:T(8,128)(2,1)} custom-call(s32[16]{0:T(128)} %bitcast.15, bf16[4,1,32,4096]{3,2,1,0:T(8,128)(2,1)} %query_ref.5, bf16[16,128,1024]{2,1,0:T(8,128)(2,1)} %bitcast.11), custom_call_target="tpu_custom_call" | custom-call | flops 268435456 | bytes 4194304 | tf_op jit(solution)/shard_map/staying_old/pallas_call | solution.py:291
  42.8 0.3 fusion
  43.2 0.1 pad_maximum_fusion
  43.3 0.0 copy-done
  43.3 0.0 copy-done.2
  43.3 0.0 copy-start.1
  43.3 1.0 %copy-done.1 = bf16[16,136,128]{2,1,0:T(8,128)(2,1)S(1)} copy-done((bf16[16,136,128]{2,1,0:T(8,128)(2,1)S(1)}, bf16[16,136,128]{2,1,0:T(8,128)(2,1)}, u32[]{:S(2)}) %copy-start.1) | copy-done | bytes 557080
  44.3 3.6 %new_part.1 = (bf16[4,1,32,4096]{3,2,1,0:T(8,128)(2,1)}, f32[32,128]{1,0:T(8,128)S(1)}) custom-call(bf16[4,1,32,4096]{3,2,1,0:T(8,128)(2,1)S(1)} %copy-done, f32[128,1024]{1,0:T(8,128)S(1)} %bitcast.8, f32[1,128,1024]{2,1,0:T(8,128)S(1)} %bitcast.9, bf16[1,1024]{1,0:T(2,128)(2,1)S(1)} %reshape.35.bias_ref, f32[128,128]{1,0:T(8,128)S(1)} %get-tuple-element.18.cos_ref, ...), custom_call_target="tpu_custom_call" | custom-call | flops 268435456 | bytes 8388608 | tf_op jit(solution)/shard_map/new_part/pallas_call | solution.py:484
  48.0 3.5 %all-to-all-done.1.old_ref = bf16[16,136,128]{2,1,0:T(8,128)(2,1)S(1)} async-done(((bf16[16,136,128]{2,1,0:T(8,128)(2,1)}), bf16[16,136,128]{2,1,0:T(8,128)(2,1)S(1)}, u32[]{:S(2)}, u32[]{:S(2)}) %all-to-all-start.1) | async-done | bytes 557088 | tf_op jit(solution)/shard_map/all_to_all | solution.py:458
  51.4 2.3 %join.1 = bf16[4,1,32,4096]{3,2,1,0:T(8,128)(2,1)} custom-call(bf16[16,136,128]{2,1,0:T(8,128)(2,1)S(1)} %all-to-all-done.1.old_ref, bf16[4,1,32,4096]{3,2,1,0:T(8,128)(2,1)} %get-tuple-element.13.new_ref, f32[32,128]{1,0:T(8,128)S(1)} %get-tuple-element.14.lse_ref), custom_call_target="tpu_custom_call", output_to_operand_aliasing={{}: (1, {})} | custom-call | flops 1048576 | bytes 2097152 | tf_op jit(solution)/shard_map/join/pallas_call | solution.py:500
  (3 shorter events, 0.0 us)
Async XLA Ops:
  1.9 21.8 %all-to-all-start = ((bf16[16,128,128]{2,1,0:T(8,128)(2,1)}), bf16[16,128,128]{2,1,0:T(8,128)(2,1)S(1)}, u32[]{:S(2)}, u32[]{:S(2)}) async-start(bf16[16,128,128]{2,1,0:T(8,128)(2,1)} %turn.1), calls=%async_computation | async-start | bytes 1048576 | tf_op jit(solution)/shard_map/all_to_all | solution.py:427
  9.2 14.5 %copy-start.3 = (s32[16,16]{1,0:T(8,128)S(1)}, s32[16,16]{1,0:T(8,128)}, u32[]{:S(2)}) copy-start(s32[16,16]{1,0:T(8,128)} %dest_ref.1) | copy-start | bytes 3076
  9.3 14.5 %copy-start.4 = (s32[16,16]{1,0:T(8,128)S(1)}, s32[16,16]{1,0:T(8,128)}, u32[]{:S(2)}) copy-start(s32[16,16]{1,0:T(8,128)} %length_ref.1) | copy-start | bytes 3076
  15.2 21.3 %copy-start.6 = (s32[1,16]{1,0:T(1,128)S(1)}, s32[1,16]{1,0:T(1,128)}, u32[]{:S(2)}) copy-start(s32[1,16]{1,0:T(1,128)} %param.14) | copy-start | bytes 196
  15.2 21.5 %copy-start.5 = (bf16[1024]{0:T(1024)(128)(2,1)S(1)}, bf16[1024]{0:T(1024)(128)(2,1)}, u32[]{:S(2)}) copy-start(bf16[1024]{0:T(1024)(128)(2,1)} %param.10) | copy-start | bytes 6148
  15.2 15.9 %collective-permute-start = (f32[128,1024]{1,0:T(8,128)}, f32[128,1024]{1,0:T(8,128)S(1)}, u32[]{:S(2)}, u32[]{:S(2)}) collective-permute-start(f32[128,1024]{1,0:T(8,128)} %bitcast.14), channel_id=1, source_target_pairs={{0,1},{1,0},{2,3},{3,2},{4,5},{5,4},{6,7},{7,6},{8,9},{9,8},{10,11... | collective-permute-start | bytes 1572872 | tf_op jit(solution)/shard_map/ppermute | solution.py:435
  22.7 20.6 %copy-start = (bf16[4,1,32,4096]{3,2,1,0:T(8,128)(2,1)S(1)}, bf16[4,1,32,4096]{3,2,1,0:T(8,128)(2,1)}, u32[]{:S(2)}) copy-start(bf16[4,1,32,4096]{3,2,1,0:T(8,128)(2,1)} %query_ref.5) | copy-start | bytes 3145732
  22.7 20.6 %copy-start.2 = (f32[1,128,1024]{2,1,0:T(8,128)S(1)}, f32[1,128,1024]{2,1,0:T(8,128)}, u32[]{:S(2)}) copy-start(f32[1,128,1024]{2,1,0:T(8,128)} %project.3) | copy-start | bytes 1572868
  31.1 20.3 %all-to-all-start.1 = ((bf16[16,136,128]{2,1,0:T(8,128)(2,1)}), bf16[16,136,128]{2,1,0:T(8,128)(2,1)S(1)}, u32[]{:S(2)}, u32[]{:S(2)}) async-start(bf16[16,136,128]{2,1,0:T(8,128)(2,1)} %moving_old.1), calls=%async_computation.1 | async-start | bytes 1114112 | tf_op jit(solution)/shard_map/all_to_all | solution.py:458
  43.3 1.1 %copy-start.1 = (bf16[16,136,128]{2,1,0:T(8,128)(2,1)S(1)}, bf16[16,136,128]{2,1,0:T(8,128)(2,1)}, u32[]{:S(2)}) copy-start(bf16[16,136,128]{2,1,0:T(8,128)(2,1)} %staying_old.1.old_ref) | copy-start | bytes 1671172

commit v4 on v3

--- a/solution.py
+++ b/solution.py
@@ -19,19 +19,30 @@
 FULL = 60 * MIB
 
 
-def cache_copy(cache_ref, buf, sems, m, rows):
-    part = pl.ds(0, rows)
-    return pltpu.make_async_copy(cache_ref.at[m, part], buf.at[m, part], sems.at[m])
+def cache_copy(cache_ref, buf, sems, m, begin, end):
+    part = pl.ds(begin, end - begin)
+    sem = sems.at[0 if begin == 0 else 1, m]
+    return pltpu.make_async_copy(cache_ref.at[m, part], buf.at[m, part], sem)
 
 
 def moving_kernel(
-    dest_ref, length_ref, query_ref, cache_ref, out_ref,
-    buf, order, answers, in_sems, out_sems, *, kv_heads,
+    dest_hbm, length_hbm, query_ref, cache_ref, out_ref,
+    buf, dest_ref, length_ref, order, answers, in_sems, out_sems, table_sems, *, kv_heads,
 ):
     count, capacity, _ = cache_ref.shape
     me = lax.axis_index("grp")
     chunk = min(capacity, 128)
     variants = capacity // chunk
+    tables = [
+        pltpu.make_async_copy(length_hbm, length_ref, table_sems.at[0]),
+        pltpu.make_async_copy(dest_hbm, dest_ref, table_sems.at[1]),
+    ]
+    for table in tables:
+        table.start()
+    for m in range(count):
+        cache_copy(cache_ref, buf, in_sems, m, 0, chunk).start()
+    for table in tables:
+        table.wait()
     used = [(length_ref[me, m] + chunk - 1) // chunk for m in range(count)]
     place = jnp.int32(0)
     for v in range(1, variants + 1):
@@ -65,6 +76,9 @@
 
     def same(m):
         return m
+
+    for m in range(count):
+        cache_copy(cache_ref, buf, sems, m, 0, min(cache_ref.shape[1], 128)).start()
 
     for k in range(kv_heads):
         turned[:, k * per : (k + 1) * per, :] = by_request(
@@ -102,35 +116,29 @@
     chunk = min(capacity, 128)
     variants = capacity // chunk
     pair = 2 if kv_heads % 2 == 0 else 1
-    part_size = [GROUP]
 
     def run(act):
-        def one(first, size):
+        @pl.loop(0, count // GROUP)
+        def _(g):
+            members = [member(g * GROUP + i) for i in range(GROUP)]
             if variants == 1:
-                act(first, size, 1)
+                act(members, 1)
                 return
-            used = (length_of(member(first + size - 1)) + chunk - 1) // chunk
+            used = (length_of(members[-1]) + chunk - 1) // chunk
             for v in range(1, variants + 1):
-                pl.when(used == v)(functools.partial(act, first, size, v))
-
-        @pl.loop(0, count // GROUP - 1)
-        def _(g):
-            one(g * GROUP, GROUP)
-
-        first = count - GROUP
-        for size in part_size:
-            one(first, size)
-            first += size
-
-    def start(first, size, v):
-        for i in range(size):
-            cache_copy(cache_ref, buf, sems, member(first + i), v * chunk).start()
-
-    def body(first, size, v):
-        length = v * chunk
-        members = [member(first + i) for i in range(size)]
+                pl.when(used == v)(functools.partial(act, members, v))
+
+    def start(members, v):
+        if v > 1:
+            for m in members:
+                cache_copy(cache_ref, buf, sems, m, chunk, v * chunk).start()
+
+    def body(members, v):
+        size, length = len(members), v * chunk
         for m in members:
-            cache_copy(cache_ref, buf, sems, m, length).wait()
+            cache_copy(cache_ref, buf, sems, m, 0, chunk).wait()
+            if v > 1:
+                cache_copy(cache_ref, buf, sems, m, chunk, length).wait()
         slots = [slot_of(m) for m in members]
         column = lax.broadcasted_iota(jnp.int32, (pair * per, length), 1)
         part = pl.ds(0, length)
@@ -191,7 +199,8 @@
             out_ref[slots[i], rows : rows + STAT, :] = terms[i]
             done(slots[i])
 
-    run(start)
+    if variants > 1:
+        run(start)
     run(body)
 
 
@@ -285,13 +294,13 @@
     )(tp_index.reshape(1), hidden, weight)
 
 
-def old_call(kernel, scalars, query, cache, rows, scratch, out_space, limit, name):
+def old_call(kernel, scalars, scalar_space, query, cache, rows, scratch, out_space, limit, name):
     count, capacity, _ = cache.shape
-    smem, vmem = pl.BlockSpec(memory_space=pltpu.SMEM), pl.BlockSpec(memory_space=pltpu.VMEM)
+    scalar, vmem = pl.BlockSpec(memory_space=scalar_space), pl.BlockSpec(memory_space=pltpu.VMEM)
     return pl.pallas_call(
         kernel,
         out_shape=jax.ShapeDtypeStruct((count, rows + STAT, HS), jnp.bfloat16),
-        in_specs=[smem] * len(scalars) + [vmem, pl.BlockSpec(memory_space=pltpu.HBM)],
+        in_specs=[scalar] * len(scalars) + [vmem, pl.BlockSpec(memory_space=pltpu.HBM)],
         out_specs=pl.BlockSpec(memory_space=out_space),
         scratch_shapes=[pltpu.VMEM(cache.shape, jnp.bfloat16)] + scratch,
         compiler_params=pltpu.CompilerParams(vmem_limit_bytes=limit),
@@ -308,15 +317,14 @@
     return stat[:, 0, :] + stat[:, 1, :] + stat[:, 2, :]
 
 
-def merge_head(old_ref, share, new_of, put, steps, per_kv, k):
+def merge_head(old_ref, share, put, steps, per_kv, k):
     per = steps * per_kv
     old = jnp.swapaxes(old_ref[:, k * per : (k + 1) * per, :], 0, 1).astype(jnp.float32)
     for s in range(steps):
         for q in range(per_kv):
             at = s * per_kv + q
             c = k * per + at
-            new = new_of(s, k * per_kv + q)
-            put(s, k * per_kv + q, new + share[:, c : c + 1] * (old[at] - new))
+            put(s, k * per_kv + q, share[:, c : c + 1] * old[at], share[:, c : c + 1])
 
 
 def new_kernel(
@@ -363,22 +371,25 @@
                 ].astype(jnp.bfloat16)
     lse_ref[...] = lse_all
 
-    def put(s, h, value):
-        out_ref[s, 0, 0:staying, h * HS : (h + 1) * HS] = value.astype(jnp.bfloat16)
-
-    def new_of(s, h):
-        return out_ref[s, 0, 0:staying, h * HS : (h + 1) * HS].astype(jnp.float32)
+    def put(s, h, old, weight):
+        lanes = pl.ds(h * HS, HS)
+        new = out_ref[s, 0, 0:staying, lanes].astype(jnp.float32)
+        out_ref[s, 0, 0:staying, lanes] = (old + (1.0 - weight) * new).astype(jnp.bfloat16)
 
     stat = old_lse(old_ref[:, rows : rows + STAT, :].astype(jnp.float32))
     share = 1.0 / (1.0 + jnp.exp(lse_all[0:staying] - stat))
     for k in range(kv_heads):
-        merge_head(old_ref, share, new_of, put, steps, per_kv, k)
-
-
-def join_kernel(old_ref, new_ref, lse_ref, out_ref, arrived, merged, in_sems, out_sems, *, kv_heads, first):
+        merge_head(old_ref, share, put, steps, per_kv, k)
+
+
+def join_kernel(
+    old_ref, new_ref, lse_ref, out_ref, arrived, weighted, weights, merged, in_sems, out_sems,
+    *, kv_heads, first,
+):
     steps = new_ref.shape[0]
     count, rows = old_ref.shape[0], old_ref.shape[1] - STAT
     width = new_ref.shape[3] // kv_heads
+    per_kv = width // HS
     own = pl.ds(first, count)
 
     def into(k):
@@ -393,17 +404,22 @@
         into(k).start()
     stat = old_lse(old_ref[:, rows : rows + STAT, :].astype(jnp.float32))
     share = 1.0 / (1.0 + jnp.exp(lse_ref[first : first + count, :] - stat))
-    for k in range(kv_heads):
-        base = k * width
-
-        def put(s, h, value):
-            merged[k, s, 0, :, h * HS - base : (h + 1) * HS - base] = value.astype(jnp.bfloat16)
-
-        def new_of(s, h):
-            return arrived[k, s, 0, :, h * HS - base : (h + 1) * HS - base].astype(jnp.float32)
-
+
+    def put(s, h, old, weight):
+        weighted[s, h] = old
+        weights[s, h] = jnp.broadcast_to(1.0 - weight, (count, HS))
+
+    for k in range(kv_heads):
+        merge_head(old_ref, share, put, steps, per_kv, k)
+    for k in range(kv_heads):
         into(k).wait()
-        merge_head(old_ref, share, new_of, put, steps, width // HS, k)
+        for s in range(steps):
+            for q in range(per_kv):
+                h, lanes = k * per_kv + q, pl.ds(q * HS, HS)
+                new = arrived[k, s, 0, :, lanes].astype(jnp.float32)
+                merged[k, s, 0, :, lanes] = (weighted[s, h] + weights[s, h] * new).astype(
+                    jnp.bfloat16
+                )
         outof(k).start()
     for k in range(kv_heads):
         outof(k).wait()
@@ -441,14 +457,18 @@
     answer = old_call(
         functools.partial(moving_kernel, kv_heads=kv_heads),
         [long_dest, long_len],
+        pltpu.HBM,
         asked,
         long_cache[0],
         rows,
         [
+            pltpu.SMEM(long_dest.shape, jnp.int32),
+            pltpu.SMEM(long_len.shape, jnp.int32),
             pltpu.SMEM((moving + 8,), jnp.int32),
             pltpu.VMEM((moving, rows + STAT, HS), jnp.bfloat16),
+            pltpu.SemaphoreType.DMA((2, moving)),
             pltpu.SemaphoreType.DMA((moving,)),
-            pltpu.SemaphoreType.DMA((moving,)),
+            pltpu.SemaphoreType.DMA((2,)),
         ],
         pltpu.HBM,
         48 * MIB,
@@ -461,10 +481,11 @@
     stayed = old_call(
         functools.partial(staying_kernel, kv_heads=kv_heads),
         [own_len],
+        pltpu.SMEM,
         queries,
         res_cache[0],
         rows,
-        [pltpu.VMEM((staying, rows, HS), jnp.bfloat16), pltpu.SemaphoreType.DMA((staying,))],
+        [pltpu.VMEM((staying, rows, HS), jnp.bfloat16), pltpu.SemaphoreType.DMA((2, staying))],
         pltpu.VMEM,
         58 * MIB,
         "staying_old",
@@ -504,6 +525,8 @@
         out_specs=hbm,
         scratch_shapes=[
             pltpu.VMEM(part, jnp.bfloat16),
+            pltpu.VMEM((step_count, head_count, moving, HS), jnp.float32),
+            pltpu.VMEM((step_count, head_count, moving, HS), jnp.float32),
             pltpu.VMEM(part, jnp.bfloat16),
             pltpu.SemaphoreType.DMA((kv_heads,)),
             pltpu.SemaphoreType.DMA((kv_heads,)),

time: 54.4 us -> 53.5 us (0.983)
  Pallas kernels: 33.2 us -> 32.5 us
where the time goes in v4:
time: 53.5 us; the launch traced here: 53.2 us
  Pallas kernels  32.5 us (61%)
  starting transfers between devices  14.6 us (27%)
  waiting for transfers between devices  4.23 us (8%)
  local copies, waits for them, and re-layouts  1.17 us (2%)
  other arithmetic  0.62 us (1%)
    pallas_call x2, Pallas kernels, old_call(): pl.pallas_call(kernel, out_shape=jax.ShapeDtypeStruct((count, rows + STAT...  13 us
    pallas_call x2, Pallas kernels, project(): pl.pallas_call(project_kernel, out_shape=jax.ShapeDtypeStruct((pieces, ro...  11.9 us
    all_to_all x1, starting transfers between devices, per_device(): lax.all_to_all(turn(queries, staying, kv_heads), 'grp', split_axis=0, con...  7.37 us
    all_to_all x1, starting transfers between devices, per_device(): lax.all_to_all(answer, 'grp', split_axis=0, concat_axis=0, tiled=True)  5.67 us
    pallas_call x1, Pallas kernels, per_device(): pl.pallas_call(functools.partial(new_kernel, kv_heads=kv_heads, per_kv=pe...  3.92 us
    all_to_all x1, waiting for transfers between devices, per_device(): lax.all_to_all(answer, 'grp', split_axis=0, concat_axis=0, tiled=True)  3.18 us
    pallas_call x1, Pallas kernels, per_device(): pl.pallas_call(functools.partial(join_kernel, kv_heads=kv_heads, first=st...  1.86 us
    pallas_call x1, Pallas kernels, turn(): pl.pallas_call(functools.partial(turn_kernel, kv_heads=kv_heads, first=fi...  1.85 us
  transfers between devices with their start and end apart: 3, of which 2 were waited for; matrix products, arithmetic and copies ran while one was open for 1% of the time, Pallas kernels for 54%

profile of v4, /device:TPU:0, one launch (start us, length us, event | category | flops | bytes accessed | tf_op | source)
XLA Modules:
  0.0 53.2 jit_solution(11095085975705800754)
XLA Ops:
  0.0 1.9 %turn.1 = bf16[16,128,128]{2,1,0:T(8,128)(2,1)} custom-call(bf16[4,1,32,4096]{3,2,1,0:T(8,128)(2,1)} %query_ref.5), custom_call_target="tpu_custom_call" | custom-call | flops 1048576 | bytes 1048576 | tf_op jit(solution)/shard_map/turn/pallas_call | solution.py:246
  1.9 7.4 %all-to-all-start = ((bf16[16,128,128]{2,1,0:T(8,128)(2,1)}), bf16[16,128,128]{2,1,0:T(8,128)(2,1)S(1)}, u32[]{:S(2)}, u32[]{:S(2)}) async-start(bf16[16,128,128]{2,1,0:T(8,128)(2,1)} %turn.1), calls=%async_computation | async-start | bytes 1048576 | tf_op jit(solution)/shard_map/all_to_all | solution.py:443
  9.2 0.0 copy-start.3
  9.3 0.0 copy-start.4
  9.3 5.9 %project.2 = f32[1,128,1024]{2,1,0:T(8,128)} custom-call(s32[1]{0:T(128)} %bitcast.1.index_ref, bf16[128,4096]{1,0:T(8,128)(2,1)} %bitcast.12, bf16[4096,2048]{1,0:T(8,128)(2,1)} %weight_ref.3), custom_call_target="tpu_custom_call" | custom-call | flops 1073741824 | bytes 8388608 | tf_op jit(solution)/shard_map/project/pallas_call | solution.py:272
  15.2 0.0 copy-start.6
  15.2 0.0 copy-start.5
  15.2 1.5 %collective-permute-start = (f32[128,1024]{1,0:T(8,128)}, f32[128,1024]{1,0:T(8,128)S(1)}, u32[]{:S(2)}, u32[]{:S(2)}) collective-permute-start(f32[128,1024]{1,0:T(8,128)} %bitcast.14), channel_id=1, source_target_pairs={{0,1},{1,0},{2,3},{3,2},{4,5},{5,4},{6,7},{7,6},{8,9},{9,8},{10,11... | collective-permute-start | bytes 1572872 | tf_op jit(solution)/shard_map/ppermute | solution.py:451
  16.7 5.9 %project.3 = f32[1,128,1024]{2,1,0:T(8,128)} custom-call(s32[1]{0:T(128)} %bitcast.1.index_ref, bf16[128,4096]{1,0:T(8,128)(2,1)} %bitcast.13, bf16[4096,2048]{1,0:T(8,128)(2,1)} %weight_ref.3), custom_call_target="tpu_custom_call" | custom-call | flops 1073741824 | bytes 8388608 | tf_op jit(solution)/shard_map/project/pallas_call | solution.py:272
  22.6 0.0 copy-start
  22.7 0.0 copy-start.2
  22.7 1.1 %all-to-all-done.query_ref = bf16[16,128,128]{2,1,0:T(8,128)(2,1)S(1)} async-done(((bf16[16,128,128]{2,1,0:T(8,128)(2,1)}), bf16[16,128,128]{2,1,0:T(8,128)(2,1)S(1)}, u32[]{:S(2)}, u32[]{:S(2)}) %all-to-all-start) | async-done | bytes 524320 | tf_op jit(solution)/shard_map/all_to_all | solution.py:443
  23.7 0.0 copy-done.3
  23.7 0.0 copy-done.4
  23.7 6.9 %moving_old.1 = bf16[16,136,128]{2,1,0:T(8,128)(2,1)} custom-call(s32[16,16]{1,0:T(8,128)S(1)} %copy-done.3, s32[16,16]{1,0:T(8,128)S(1)} %copy-done.4, bf16[16,128,128]{2,1,0:T(8,128)(2,1)S(1)} %all-to-all-done.query_ref, bf16[16,512,1024]{2,1,0:T(8,128)(2,1)} %bitcast.10), custom_call_target="tpu_custom_call" | custom-call | flops 1073741824 | bytes 16777216 | tf_op jit(solution)/shard_map/moving_old/pallas_call | solution.py:300
  30.6 0.0 collective-permute-done
  30.6 5.7 %all-to-all-start.1 = ((bf16[16,136,128]{2,1,0:T(8,128)(2,1)}), bf16[16,136,128]{2,1,0:T(8,128)(2,1)S(1)}, u32[]{:S(2)}, u32[]{:S(2)}) async-start(bf16[16,136,128]{2,1,0:T(8,128)(2,1)} %moving_old.1), calls=%async_computation.1 | async-start | bytes 1114112 | tf_op jit(solution)/shard_map/all_to_all | solution.py:478
  36.3 0.1 select_reduce_fusion
  36.4 0.0 copy-done.6
  36.4 0.1 pad_add_fusion
  36.5 0.1 convert_element_type.13
  36.6 0.0 copy-done.5
  36.6 6.1 %staying_old.1.old_ref = bf16[16,136,128]{2,1,0:T(8,128)(2,1)} custom-call(s32[16]{0:T(128)} %bitcast.15, bf16[4,1,32,4096]{3,2,1,0:T(8,128)(2,1)} %query_ref.5, bf16[16,128,1024]{2,1,0:T(8,128)(2,1)} %bitcast.11), custom_call_target="tpu_custom_call" | custom-call | flops 268435456 | bytes 4194304 | tf_op jit(solution)/shard_map/staying_old/pallas_call | solution.py:300
  42.7 0.3 fusion
  43.1 0.1 pad_maximum_fusion
  43.2 0.0 copy-done
  43.2 0.0 copy-done.2
  43.2 0.0 copy-start.1
  43.2 1.0 %copy-done.1 = bf16[16,136,128]{2,1,0:T(8,128)(2,1)S(1)} copy-done((bf16[16,136,128]{2,1,0:T(8,128)(2,1)S(1)}, bf16[16,136,128]{2,1,0:T(8,128)(2,1)}, u32[]{:S(2)}) %copy-start.1) | copy-done | bytes 557080
  44.2 3.9 %new_part.1 = (bf16[4,1,32,4096]{3,2,1,0:T(8,128)(2,1)}, f32[32,128]{1,0:T(8,128)S(1)}) custom-call(bf16[4,1,32,4096]{3,2,1,0:T(8,128)(2,1)S(1)} %copy-done, f32[128,1024]{1,0:T(8,128)S(1)} %bitcast.8, f32[1,128,1024]{2,1,0:T(8,128)S(1)} %bitcast.9, bf16[1,1024]{1,0:T(2,128)(2,1)S(1)} %reshape.35.bias_ref, f32[128,128]{1,0:T(8,128)S(1)} %get-tuple-element.18.cos_ref, ...), custom_call_target="tpu_custom_call" | custom-call | flops 268435456 | bytes 8388608 | tf_op jit(solution)/shard_map/new_part/pallas_call | solution.py:505
  48.2 3.2 %all-to-all-done.1.old_ref = bf16[16,136,128]{2,1,0:T(8,128)(2,1)S(1)} async-done(((bf16[16,136,128]{2,1,0:T(8,128)(2,1)}), bf16[16,136,128]{2,1,0:T(8,128)(2,1)S(1)}, u32[]{:S(2)}, u32[]{:S(2)}) %all-to-all-start.1) | async-done | bytes 557088 | tf_op jit(solution)/shard_map/all_to_all | solution.py:478
  51.3 1.9 %join.1 = bf16[4,1,32,4096]{3,2,1,0:T(8,128)(2,1)} custom-call(bf16[16,136,128]{2,1,0:T(8,128)(2,1)S(1)} %all-to-all-done.1.old_ref, bf16[4,1,32,4096]{3,2,1,0:T(8,128)(2,1)} %get-tuple-element.13.new_ref, f32[32,128]{1,0:T(8,128)S(1)} %get-tuple-element.14.lse_ref), custom_call_target="tpu_custom_call", output_to_operand_aliasing={{}: (1, {})} | custom-call | flops 1048576 | bytes 2097152 | tf_op jit(solution)/shard_map/join/pallas_call | solution.py:521
  (3 shorter events, 0.0 us)
Async XLA Ops:
  1.9 21.8 %all-to-all-start = ((bf16[16,128,128]{2,1,0:T(8,128)(2,1)}), bf16[16,128,128]{2,1,0:T(8,128)(2,1)S(1)}, u32[]{:S(2)}, u32[]{:S(2)}) async-start(bf16[16,128,128]{2,1,0:T(8,128)(2,1)} %turn.1), calls=%async_computation | async-start | bytes 1048576 | tf_op jit(solution)/shard_map/all_to_all | solution.py:443
  9.2 14.5 %copy-start.3 = (s32[16,16]{1,0:T(8,128)S(1)}, s32[16,16]{1,0:T(8,128)}, u32[]{:S(2)}) copy-start(s32[16,16]{1,0:T(8,128)} %dest_hbm.1) | copy-start | bytes 3076
  9.3 14.5 %copy-start.4 = (s32[16,16]{1,0:T(8,128)S(1)}, s32[16,16]{1,0:T(8,128)}, u32[]{:S(2)}) copy-start(s32[16,16]{1,0:T(8,128)} %length_hbm.1) | copy-start | bytes 3076
  15.2 21.2 %copy-start.6 = (s32[1,16]{1,0:T(1,128)S(1)}, s32[1,16]{1,0:T(1,128)}, u32[]{:S(2)}) copy-start(s32[1,16]{1,0:T(1,128)} %param.14) | copy-start | bytes 196
  15.2 21.4 %copy-start.5 = (bf16[1024]{0:T(1024)(128)(2,1)S(1)}, bf16[1024]{0:T(1024)(128)(2,1)}, u32[]{:S(2)}) copy-start(bf16[1024]{0:T(1024)(128)(2,1)} %param.10) | copy-start | bytes 6148
  15.2 15.4 %collective-permute-start = (f32[128,1024]{1,0:T(8,128)}, f32[128,1024]{1,0:T(8,128)S(1)}, u32[]{:S(2)}, u32[]{:S(2)}) collective-permute-start(f32[128,1024]{1,0:T(8,128)} %bitcast.14), channel_id=1, source_target_pairs={{0,1},{1,0},{2,3},{3,2},{4,5},{5,4},{6,7},{7,6},{8,9},{9,8},{10,11... | collective-permute-start | bytes 1572872 | tf_op jit(solution)/shard_map/ppermute | solution.py:451
  22.6 20.5 %copy-start = (bf16[4,1,32,4096]{3,2,1,0:T(8,128)(2,1)S(1)}, bf16[4,1,32,4096]{3,2,1,0:T(8,128)(2,1)}, u32[]{:S(2)}) copy-start(bf16[4,1,32,4096]{3,2,1,0:T(8,128)(2,1)} %query_ref.5) | copy-start | bytes 3145732
  22.7 20.5 %copy-start.2 = (f32[1,128,1024]{2,1,0:T(8,128)S(1)}, f32[1,128,1024]{2,1,0:T(8,128)}, u32[]{:S(2)}) copy-start(f32[1,128,1024]{2,1,0:T(8,128)} %project.3) | copy-start | bytes 1572868
  30.6 20.7 %all-to-all-start.1 = ((bf16[16,136,128]{2,1,0:T(8,128)(2,1)}), bf16[16,136,128]{2,1,0:T(8,128)(2,1)S(1)}, u32[]{:S(2)}, u32[]{:S(2)}) async-start(bf16[16,136,128]{2,1,0:T(8,128)(2,1)} %moving_old.1), calls=%async_computation.1 | async-start | bytes 1114112 | tf_op jit(solution)/shard_map/all_to_all | solution.py:478
  43.2 1.1 %copy-start.1 = (bf16[16,136,128]{2,1,0:T(8,128)(2,1)S(1)}, bf16[16,136,128]{2,1,0:T(8,128)(2,1)}, u32[]{:S(2)}) copy-start(bf16[16,136,128]{2,1,0:T(8,128)(2,1)} %staying_old.1.old_ref) | copy-start | bytes 1671172

commit v5 on v4

--- a/solution.py
+++ b/solution.py
@@ -267,7 +267,7 @@
 
 def project(hidden, weight, kv_cols, tp_size, tp_index, first, pieces):
     rows, depth = hidden.shape
-    width = min(kv_cols, 256)
+    width = min(kv_cols, 512)
     blocks = kv_cols // width
     return pl.pallas_call(
         project_kernel,

time: 53.5 us -> 52.2 us (0.976)
  starting transfers between devices: 14.6 us -> 12.9 us
  waiting for transfers between devices: 4.23 us -> 5.59 us
  Pallas kernels: 32.5 us -> 31.2 us
    all_to_all x1, starting transfers between devices: 5.67 us -> 4.04 us  [per_device(): lax.all_to_all(answer, 'grp', split_axis=0, concat_axis=0, tiled=True)]
    pallas_call x2, Pallas kernels: 11.9 us -> 10.5 us  [project(): pl.pallas_call(project_kernel, out_shape=jax.ShapeDtypeStruct((pieces, ro...]
    all_to_all x1, waiting for transfers between devices: 1.05 us -> 2.41 us  [per_device(): lax.all_to_all(turn(queries, staying, kv_heads), 'grp', split_axis=0, con...]
  transfers between devices with their start and end apart: 3 -> 3, of which waited for: 2 -> 2; matrix products, arithmetic and copies ran while one was open for 1% -> 1% of each run, Pallas kernels for 54% -> 53%
where the time goes in v5:
time: 52.2 us; the launch traced here: 51.6 us
  Pallas kernels  31.2 us (60%)
  starting transfers between devices  12.9 us (25%)
  waiting for transfers between devices  5.59 us (11%)
  local copies, waits for them, and re-layouts  1.17 us (2%)
  other arithmetic  0.62 us (1%)
    pallas_call x2, Pallas kernels, old_call(): pl.pallas_call(kernel, out_shape=jax.ShapeDtypeStruct((count, rows + STAT...  13 us
    pallas_call x2, Pallas kernels, project(): pl.pallas_call(project_kernel, out_shape=jax.ShapeDtypeStruct((pieces, ro...  10.5 us
    all_to_all x1, starting transfers between devices, per_device(): lax.all_to_all(turn(queries, staying, kv_heads), 'grp', split_axis=0, con...  7.37 us
    all_to_all x1, starting transfers between devices, per_device(): lax.all_to_all(answer, 'grp', split_axis=0, concat_axis=0, tiled=True)  4.04 us
    pallas_call x1, Pallas kernels, per_device(): pl.pallas_call(functools.partial(new_kernel, kv_heads=kv_heads, per_kv=pe...  3.92 us
    all_to_all x1, waiting for transfers between devices, per_device(): lax.all_to_all(answer, 'grp', split_axis=0, concat_axis=0, tiled=True)  3.18 us
    all_to_all x1, waiting for transfers between devices, per_device(): lax.all_to_all(turn(queries, staying, kv_heads), 'grp', split_axis=0, con...  2.41 us
    pallas_call x1, Pallas kernels, per_device(): pl.pallas_call(functools.partial(join_kernel, kv_heads=kv_heads, first=st...  1.86 us
  transfers between devices with their start and end apart: 3, of which 2 were waited for; matrix products, arithmetic and copies ran while one was open for 1% of the time, Pallas kernels for 53%

profile of v5, /device:TPU:0, one launch (start us, length us, event | category | flops | bytes accessed | tf_op | source)
XLA Modules:
  0.0 51.6 jit_solution(8819359458804350375)
XLA Ops:
  0.0 1.9 %turn.1 = bf16[16,128,128]{2,1,0:T(8,128)(2,1)} custom-call(bf16[4,1,32,4096]{3,2,1,0:T(8,128)(2,1)} %query_ref.5), custom_call_target="tpu_custom_call" | custom-call | flops 1048576 | bytes 1048576 | tf_op jit(solution)/shard_map/turn/pallas_call | solution.py:246
  1.9 7.4 %all-to-all-start = ((bf16[16,128,128]{2,1,0:T(8,128)(2,1)}), bf16[16,128,128]{2,1,0:T(8,128)(2,1)S(1)}, u32[]{:S(2)}, u32[]{:S(2)}) async-start(bf16[16,128,128]{2,1,0:T(8,128)(2,1)} %turn.1), calls=%async_computation | async-start | bytes 1048576 | tf_op jit(solution)/shard_map/all_to_all | solution.py:443
  9.2 0.0 copy-start.3
  9.3 0.0 copy-start.4
  9.3 5.2 %project.2 = f32[1,128,1024]{2,1,0:T(8,128)} custom-call(s32[1]{0:T(128)} %bitcast.1.index_ref, bf16[128,4096]{1,0:T(8,128)(2,1)} %bitcast.12, bf16[4096,2048]{1,0:T(8,128)(2,1)} %weight_ref.3), custom_call_target="tpu_custom_call" | custom-call | flops 1073741824 | bytes 8388608 | tf_op jit(solution)/shard_map/project/pallas_call | solution.py:272
  14.5 0.0 copy-start.6
  14.5 0.0 copy-start.5
  14.5 1.5 %collective-permute-start = (f32[128,1024]{1,0:T(8,128)}, f32[128,1024]{1,0:T(8,128)S(1)}, u32[]{:S(2)}, u32[]{:S(2)}) collective-permute-start(f32[128,1024]{1,0:T(8,128)} %bitcast.14), channel_id=1, source_target_pairs={{0,1},{1,0},{2,3},{3,2},{4,5},{5,4},{6,7},{7,6},{8,9},{9,8},{10,11... | collective-permute-start | bytes 1572872 | tf_op jit(solution)/shard_map/ppermute | solution.py:451
  16.0 5.3 %project.3 = f32[1,128,1024]{2,1,0:T(8,128)} custom-call(s32[1]{0:T(128)} %bitcast.1.index_ref, bf16[128,4096]{1,0:T(8,128)(2,1)} %bitcast.13, bf16[4096,2048]{1,0:T(8,128)(2,1)} %weight_ref.3), custom_call_target="tpu_custom_call" | custom-call | flops 1073741824 | bytes 8388608 | tf_op jit(solution)/shard_map/project/pallas_call | solution.py:272
  21.3 0.0 copy-start
  21.3 0.0 copy-start.2
  21.3 2.4 %all-to-all-done.query_ref = bf16[16,128,128]{2,1,0:T(8,128)(2,1)S(1)} async-done(((bf16[16,128,128]{2,1,0:T(8,128)(2,1)}), bf16[16,128,128]{2,1,0:T(8,128)(2,1)S(1)}, u32[]{:S(2)}, u32[]{:S(2)}) %all-to-all-start) | async-done | bytes 524320 | tf_op jit(solution)/shard_map/all_to_all | solution.py:443
  23.7 0.0 copy-done.3
  23.7 0.0 copy-done.4
  23.7 6.9 %moving_old.1 = bf16[16,136,128]{2,1,0:T(8,128)(2,1)} custom-call(s32[16,16]{1,0:T(8,128)S(1)} %copy-done.3, s32[16,16]{1,0:T(8,128)S(1)} %copy-done.4, bf16[16,128,128]{2,1,0:T(8,128)(2,1)S(1)} %all-to-all-done.query_ref, bf16[16,512,1024]{2,1,0:T(8,128)(2,1)} %bitcast.10), custom_call_target="tpu_custom_call" | custom-call | flops 1073741824 | bytes 16777216 | tf_op jit(solution)/shard_map/moving_old/pallas_call | solution.py:300
  30.7 0.0 collective-permute-done
  30.7 4.0 %all-to-all-start.1 = ((bf16[16,136,128]{2,1,0:T(8,128)(2,1)}), bf16[16,136,128]{2,1,0:T(8,128)(2,1)S(1)}, u32[]{:S(2)}, u32[]{:S(2)}) async-start(bf16[16,136,128]{2,1,0:T(8,128)(2,1)} %moving_old.1), calls=%async_computation.1 | async-start | bytes 1114112 | tf_op jit(solution)/shard_map/all_to_all | solution.py:478
  34.7 0.1 select_reduce_fusion
  34.8 0.0 copy-done.6
  34.8 0.1 pad_add_fusion
  34.9 0.1 convert_element_type.13
  35.0 0.0 copy-done.5
  35.0 6.1 %staying_old.1.old_ref = bf16[16,136,128]{2,1,0:T(8,128)(2,1)} custom-call(s32[16]{0:T(128)} %bitcast.15, bf16[4,1,32,4096]{3,2,1,0:T(8,128)(2,1)} %query_ref.5, bf16[16,128,1024]{2,1,0:T(8,128)(2,1)} %bitcast.11), custom_call_target="tpu_custom_call" | custom-call | flops 268435456 | bytes 4194304 | tf_op jit(solution)/shard_map/staying_old/pallas_call | solution.py:300
  41.1 0.3 fusion
  41.5 0.1 pad_maximum_fusion
  41.6 0.0 copy-done
  41.6 0.0 copy-done.2
  41.6 0.0 copy-start.1
  41.6 1.0 %copy-done.1 = bf16[16,136,128]{2,1,0:T(8,128)(2,1)S(1)} copy-done((bf16[16,136,128]{2,1,0:T(8,128)(2,1)S(1)}, bf16[16,136,128]{2,1,0:T(8,128)(2,1)}, u32[]{:S(2)}) %copy-start.1) | copy-done | bytes 557080
  42.7 3.9 %new_part.1 = (bf16[4,1,32,4096]{3,2,1,0:T(8,128)(2,1)}, f32[32,128]{1,0:T(8,128)S(1)}) custom-call(bf16[4,1,32,4096]{3,2,1,0:T(8,128)(2,1)S(1)} %copy-done, f32[128,1024]{1,0:T(8,128)S(1)} %bitcast.8, f32[1,128,1024]{2,1,0:T(8,128)S(1)} %bitcast.9, bf16[1,1024]{1,0:T(2,128)(2,1)S(1)} %reshape.35.bias_ref, f32[128,128]{1,0:T(8,128)S(1)} %get-tuple-element.18.cos_ref, ...), custom_call_target="tpu_custom_call" | custom-call | flops 268435456 | bytes 8388608 | tf_op jit(solution)/shard_map/new_part/pallas_call | solution.py:505
  46.6 3.2 %all-to-all-done.1.old_ref = bf16[16,136,128]{2,1,0:T(8,128)(2,1)S(1)} async-done(((bf16[16,136,128]{2,1,0:T(8,128)(2,1)}), bf16[16,136,128]{2,1,0:T(8,128)(2,1)S(1)}, u32[]{:S(2)}, u32[]{:S(2)}) %all-to-all-start.1) | async-done | bytes 557088 | tf_op jit(solution)/shard_map/all_to_all | solution.py:478
  49.7 1.9 %join.1 = bf16[4,1,32,4096]{3,2,1,0:T(8,128)(2,1)} custom-call(bf16[16,136,128]{2,1,0:T(8,128)(2,1)S(1)} %all-to-all-done.1.old_ref, bf16[4,1,32,4096]{3,2,1,0:T(8,128)(2,1)} %get-tuple-element.13.new_ref, f32[32,128]{1,0:T(8,128)S(1)} %get-tuple-element.14.lse_ref), custom_call_target="tpu_custom_call", output_to_operand_aliasing={{}: (1, {})} | custom-call | flops 1048576 | bytes 2097152 | tf_op jit(solution)/shard_map/join/pallas_call | solution.py:521
  (3 shorter events, 0.0 us)
Async XLA Ops:
  1.9 21.8 %all-to-all-start = ((bf16[16,128,128]{2,1,0:T(8,128)(2,1)}), bf16[16,128,128]{2,1,0:T(8,128)(2,1)S(1)}, u32[]{:S(2)}, u32[]{:S(2)}) async-start(bf16[16,128,128]{2,1,0:T(8,128)(2,1)} %turn.1), calls=%async_computation | async-start | bytes 1048576 | tf_op jit(solution)/shard_map/all_to_all | solution.py:443
  9.2 14.5 %copy-start.3 = (s32[16,16]{1,0:T(8,128)S(1)}, s32[16,16]{1,0:T(8,128)}, u32[]{:S(2)}) copy-start(s32[16,16]{1,0:T(8,128)} %dest_hbm.1) | copy-start | bytes 3076
  9.3 14.5 %copy-start.4 = (s32[16,16]{1,0:T(8,128)S(1)}, s32[16,16]{1,0:T(8,128)}, u32[]{:S(2)}) copy-start(s32[16,16]{1,0:T(8,128)} %length_hbm.1) | copy-start | bytes 3076
  14.5 20.3 %copy-start.6 = (s32[1,16]{1,0:T(1,128)S(1)}, s32[1,16]{1,0:T(1,128)}, u32[]{:S(2)}) copy-start(s32[1,16]{1,0:T(1,128)} %param.14) | copy-start | bytes 196
  14.5 20.5 %copy-start.5 = (bf16[1024]{0:T(1024)(128)(2,1)S(1)}, bf16[1024]{0:T(1024)(128)(2,1)}, u32[]{:S(2)}) copy-start(bf16[1024]{0:T(1024)(128)(2,1)} %param.10) | copy-start | bytes 6148
  14.5 16.2 %collective-permute-start = (f32[128,1024]{1,0:T(8,128)}, f32[128,1024]{1,0:T(8,128)S(1)}, u32[]{:S(2)}, u32[]{:S(2)}) collective-permute-start(f32[128,1024]{1,0:T(8,128)} %bitcast.14), channel_id=1, source_target_pairs={{0,1},{1,0},{2,3},{3,2},{4,5},{5,4},{6,7},{7,6},{8,9},{9,8},{10,11... | collective-permute-start | bytes 1572872 | tf_op jit(solution)/shard_map/ppermute | solution.py:451
  21.3 20.3 %copy-start = (bf16[4,1,32,4096]{3,2,1,0:T(8,128)(2,1)S(1)}, bf16[4,1,32,4096]{3,2,1,0:T(8,128)(2,1)}, u32[]{:S(2)}) copy-start(bf16[4,1,32,4096]{3,2,1,0:T(8,128)(2,1)} %query_ref.5) | copy-start | bytes 3145732
  21.3 20.3 %copy-start.2 = (f32[1,128,1024]{2,1,0:T(8,128)S(1)}, f32[1,128,1024]{2,1,0:T(8,128)}, u32[]{:S(2)}) copy-start(f32[1,128,1024]{2,1,0:T(8,128)} %project.3) | copy-start | bytes 1572868
  30.7 19.1 %all-to-all-start.1 = ((bf16[16,136,128]{2,1,0:T(8,128)(2,1)}), bf16[16,136,128]{2,1,0:T(8,128)(2,1)S(1)}, u32[]{:S(2)}, u32[]{:S(2)}) async-start(bf16[16,136,128]{2,1,0:T(8,128)(2,1)} %moving_old.1), calls=%async_computation.1 | async-start | bytes 1114112 | tf_op jit(solution)/shard_map/all_to_all | solution.py:478
  41.6 1.1 %copy-start.1 = (bf16[16,136,128]{2,1,0:T(8,128)(2,1)S(1)}, bf16[16,136,128]{2,1,0:T(8,128)(2,1)}, u32[]{:S(2)}) copy-start(bf16[16,136,128]{2,1,0:T(8,128)(2,1)} %staying_old.1.old_ref) | copy-start | bytes 1671172

commit v6 on v5

--- a/solution.py
+++ b/solution.py
@@ -128,17 +128,49 @@
             for v in range(1, variants + 1):
                 pl.when(used == v)(functools.partial(act, members, v))
 
+    def chunks(m):
+        return (length_of(m) + chunk - 1) // chunk
+
+    def rest(members, v, act, unread):
+        if v == 1:
+            return
+        uniform = chunks(members[0]) == v
+
+        @pl.when(uniform)
+        def _():
+            for m in members:
+                act(cache_copy(cache_ref, buf, sems, m, chunk, v * chunk))
+
+        @pl.when(jnp.logical_not(uniform))
+        def _():
+            for m in members:
+                own = chunks(m)
+
+                @pl.loop(1, own)
+                def _(c):
+                    part = pl.ds(pl.multiple_of(c * chunk, chunk), chunk)
+                    act(
+                        pltpu.make_async_copy(
+                            cache_ref.at[m, part], buf.at[m, part], sems.at[1, m]
+                        )
+                    )
+
+                pl.loop(own, v)(functools.partial(unread, m))
+
+    def clear(m, c):
+        part = pl.ds(pl.multiple_of(c * chunk, chunk), chunk)
+        for h in range(kv_heads):
+            lanes = pl.ds((2 * h + 1) * HS, HS)
+            buf[m, part, lanes] = jnp.zeros((chunk, HS), jnp.bfloat16)
+
     def start(members, v):
-        if v > 1:
-            for m in members:
-                cache_copy(cache_ref, buf, sems, m, chunk, v * chunk).start()
+        rest(members, v, lambda c: c.start(), clear)
 
     def body(members, v):
         size, length = len(members), v * chunk
         for m in members:
             cache_copy(cache_ref, buf, sems, m, 0, chunk).wait()
-            if v > 1:
-                cache_copy(cache_ref, buf, sems, m, chunk, length).wait()
+        rest(members, v, lambda c: c.wait(), lambda m, c: None)
         slots = [slot_of(m) for m in members]
         column = lax.broadcasted_iota(jnp.int32, (pair * per, length), 1)
         part = pl.ds(0, length)

time: 52.2 us -> 52.3 us (level)
  no operation moved by 1% of the time
where the time goes in v6:
time: 52.3 us; the launch traced here: 51.9 us
  Pallas kernels  31.1 us (59%)
  starting transfers between devices  13.2 us (25%)
  waiting for transfers between devices  5.59 us (11%)
  local copies, waits for them, and re-layouts  1.17 us (2%)
  other arithmetic  0.62 us (1%)
    pallas_call x2, Pallas kernels, old_call(): pl.pallas_call(kernel, out_shape=jax.ShapeDtypeStruct((count, rows + STAT...  13 us
    pallas_call x2, Pallas kernels, project(): pl.pallas_call(project_kernel, out_shape=jax.ShapeDtypeStruct((pieces, ro...  10.5 us
    all_to_all x1, starting transfers between devices, per_device(): lax.all_to_all(turn(queries, staying, kv_heads), 'grp', split_axis=0, con...  7.37 us
    all_to_all x1, starting transfers between devices, per_device(): lax.all_to_all(answer, 'grp', split_axis=0, concat_axis=0, tiled=True)  4.31 us
    pallas_call x1, Pallas kernels, per_device(): pl.pallas_call(functools.partial(new_kernel, kv_heads=kv_heads, per_kv=pe...  3.92 us
    all_to_all x1, waiting for transfers between devices, per_device(): lax.all_to_all(answer, 'grp', split_axis=0, concat_axis=0, tiled=True)  3.18 us
    all_to_all x1, waiting for transfers between devices, per_device(): lax.all_to_all(turn(queries, staying, kv_heads), 'grp', split_axis=0, con...  2.41 us
    pallas_call x1, Pallas kernels, per_device(): pl.pallas_call(functools.partial(join_kernel, kv_heads=kv_heads, first=st...  1.86 us
  transfers between devices with their start and end apart: 3, of which 2 were waited for; matrix products, arithmetic and copies ran while one was open for 1% of the time, Pallas kernels for 53%

profile of v6, /device:TPU:0, one launch (start us, length us, event | category | flops | bytes accessed | tf_op | source)
XLA Modules:
  0.0 51.9 jit_solution(4897674547742670946)
XLA Ops:
  0.0 1.9 %turn.1 = bf16[16,128,128]{2,1,0:T(8,128)(2,1)} custom-call(bf16[4,1,32,4096]{3,2,1,0:T(8,128)(2,1)} %query_ref.5), custom_call_target="tpu_custom_call" | custom-call | flops 1048576 | bytes 1048576 | tf_op jit(solution)/shard_map/turn/pallas_call | solution.py:278
  1.9 7.4 %all-to-all-start = ((bf16[16,128,128]{2,1,0:T(8,128)(2,1)}), bf16[16,128,128]{2,1,0:T(8,128)(2,1)S(1)}, u32[]{:S(2)}, u32[]{:S(2)}) async-start(bf16[16,128,128]{2,1,0:T(8,128)(2,1)} %turn.1), calls=%async_computation | async-start | bytes 1048576 | tf_op jit(solution)/shard_map/all_to_all | solution.py:475
  9.2 0.0 copy-start.3
  9.3 0.0 copy-start.4
  9.3 5.2 %project.2 = f32[1,128,1024]{2,1,0:T(8,128)} custom-call(s32[1]{0:T(128)} %bitcast.1.index_ref, bf16[128,4096]{1,0:T(8,128)(2,1)} %bitcast.12, bf16[4096,2048]{1,0:T(8,128)(2,1)} %weight_ref.3), custom_call_target="tpu_custom_call" | custom-call | flops 1073741824 | bytes 8388608 | tf_op jit(solution)/shard_map/project/pallas_call | solution.py:304
  14.5 0.0 copy-start.6
  14.5 0.0 copy-start.5
  14.5 1.5 %collective-permute-start = (f32[128,1024]{1,0:T(8,128)}, f32[128,1024]{1,0:T(8,128)S(1)}, u32[]{:S(2)}, u32[]{:S(2)}) collective-permute-start(f32[128,1024]{1,0:T(8,128)} %bitcast.14), channel_id=1, source_target_pairs={{0,1},{1,0},{2,3},{3,2},{4,5},{5,4},{6,7},{7,6},{8,9},{9,8},{10,11... | collective-permute-start | bytes 1572872 | tf_op jit(solution)/shard_map/ppermute | solution.py:483
  16.0 5.3 %project.3 = f32[1,128,1024]{2,1,0:T(8,128)} custom-call(s32[1]{0:T(128)} %bitcast.1.index_ref, bf16[128,4096]{1,0:T(8,128)(2,1)} %bitcast.13, bf16[4096,2048]{1,0:T(8,128)(2,1)} %weight_ref.3), custom_call_target="tpu_custom_call" | custom-call | flops 1073741824 | bytes 8388608 | tf_op jit(solution)/shard_map/project/pallas_call | solution.py:304
  21.3 0.0 copy-start
  21.3 0.0 copy-start.2
  21.3 2.4 %all-to-all-done.query_ref = bf16[16,128,128]{2,1,0:T(8,128)(2,1)S(1)} async-done(((bf16[16,128,128]{2,1,0:T(8,128)(2,1)}), bf16[16,128,128]{2,1,0:T(8,128)(2,1)S(1)}, u32[]{:S(2)}, u32[]{:S(2)}) %all-to-all-start) | async-done | bytes 524320 | tf_op jit(solution)/shard_map/all_to_all | solution.py:475
  23.7 0.0 copy-done.3
  23.7 0.0 copy-done.4
  23.7 6.9 %moving_old.1 = bf16[16,136,128]{2,1,0:T(8,128)(2,1)} custom-call(s32[16,16]{1,0:T(8,128)S(1)} %copy-done.3, s32[16,16]{1,0:T(8,128)S(1)} %copy-done.4, bf16[16,128,128]{2,1,0:T(8,128)(2,1)S(1)} %all-to-all-done.query_ref, bf16[16,512,1024]{2,1,0:T(8,128)(2,1)} %bitcast.10), custom_call_target="tpu_custom_call" | custom-call | flops 1073741824 | bytes 16777216 | tf_op jit(solution)/shard_map/moving_old/pallas_call | solution.py:332
  30.6 0.0 collective-permute-done
  30.7 4.3 %all-to-all-start.1 = ((bf16[16,136,128]{2,1,0:T(8,128)(2,1)}), bf16[16,136,128]{2,1,0:T(8,128)(2,1)S(1)}, u32[]{:S(2)}, u32[]{:S(2)}) async-start(bf16[16,136,128]{2,1,0:T(8,128)(2,1)} %moving_old.1), calls=%async_computation.1 | async-start | bytes 1114112 | tf_op jit(solution)/shard_map/all_to_all | solution.py:510
  35.0 0.1 select_reduce_fusion
  35.1 0.0 copy-done.6
  35.1 0.1 pad_add_fusion
  35.2 0.1 convert_element_type.13
  35.3 0.0 copy-done.5
  35.3 6.1 %staying_old.1.old_ref = bf16[16,136,128]{2,1,0:T(8,128)(2,1)} custom-call(s32[16]{0:T(128)} %bitcast.15, bf16[4,1,32,4096]{3,2,1,0:T(8,128)(2,1)} %query_ref.5, bf16[16,128,1024]{2,1,0:T(8,128)(2,1)} %bitcast.11), custom_call_target="tpu_custom_call" | custom-call | flops 268435456 | bytes 4194304 | tf_op jit(solution)/shard_map/staying_old/pallas_call | solution.py:332
  41.4 0.3 fusion
  41.7 0.1 pad_maximum_fusion
  41.8 0.0 copy-done
  41.8 0.0 copy-done.2
  41.8 0.0 copy-start.1
  41.9 1.0 %copy-done.1 = bf16[16,136,128]{2,1,0:T(8,128)(2,1)S(1)} copy-done((bf16[16,136,128]{2,1,0:T(8,128)(2,1)S(1)}, bf16[16,136,128]{2,1,0:T(8,128)(2,1)}, u32[]{:S(2)}) %copy-start.1) | copy-done | bytes 557080
  42.9 3.9 %new_part.1 = (bf16[4,1,32,4096]{3,2,1,0:T(8,128)(2,1)}, f32[32,128]{1,0:T(8,128)S(1)}) custom-call(bf16[4,1,32,4096]{3,2,1,0:T(8,128)(2,1)S(1)} %copy-done, f32[128,1024]{1,0:T(8,128)S(1)} %bitcast.8, f32[1,128,1024]{2,1,0:T(8,128)S(1)} %bitcast.9, bf16[1,1024]{1,0:T(2,128)(2,1)S(1)} %reshape.35.bias_ref, f32[128,128]{1,0:T(8,128)S(1)} %get-tuple-element.18.cos_ref, ...), custom_call_target="tpu_custom_call" | custom-call | flops 268435456 | bytes 8388608 | tf_op jit(solution)/shard_map/new_part/pallas_call | solution.py:537
  46.8 3.2 %all-to-all-done.1.old_ref = bf16[16,136,128]{2,1,0:T(8,128)(2,1)S(1)} async-done(((bf16[16,136,128]{2,1,0:T(8,128)(2,1)}), bf16[16,136,128]{2,1,0:T(8,128)(2,1)S(1)}, u32[]{:S(2)}, u32[]{:S(2)}) %all-to-all-start.1) | async-done | bytes 557088 | tf_op jit(solution)/shard_map/all_to_all | solution.py:510
  50.0 1.9 %join.1 = bf16[4,1,32,4096]{3,2,1,0:T(8,128)(2,1)} custom-call(bf16[16,136,128]{2,1,0:T(8,128)(2,1)S(1)} %all-to-all-done.1.old_ref, bf16[4,1,32,4096]{3,2,1,0:T(8,128)(2,1)} %get-tuple-element.13.new_ref, f32[32,128]{1,0:T(8,128)S(1)} %get-tuple-element.14.lse_ref), custom_call_target="tpu_custom_call", output_to_operand_aliasing={{}: (1, {})} | custom-call | flops 1048576 | bytes 2097152 | tf_op jit(solution)/shard_map/join/pallas_call | solution.py:553
  (3 shorter events, 0.0 us)
Async XLA Ops:
  1.9 21.8 %all-to-all-start = ((bf16[16,128,128]{2,1,0:T(8,128)(2,1)}), bf16[16,128,128]{2,1,0:T(8,128)(2,1)S(1)}, u32[]{:S(2)}, u32[]{:S(2)}) async-start(bf16[16,128,128]{2,1,0:T(8,128)(2,1)} %turn.1), calls=%async_computation | async-start | bytes 1048576 | tf_op jit(solution)/shard_map/all_to_all | solution.py:475
  9.2 14.5 %copy-start.3 = (s32[16,16]{1,0:T(8,128)S(1)}, s32[16,16]{1,0:T(8,128)}, u32[]{:S(2)}) copy-start(s32[16,16]{1,0:T(8,128)} %dest_hbm.1) | copy-start | bytes 3076
  9.3 14.5 %copy-start.4 = (s32[16,16]{1,0:T(8,128)S(1)}, s32[16,16]{1,0:T(8,128)}, u32[]{:S(2)}) copy-start(s32[16,16]{1,0:T(8,128)} %length_hbm.1) | copy-start | bytes 3076
  14.5 20.6 %copy-start.6 = (s32[1,16]{1,0:T(1,128)S(1)}, s32[1,16]{1,0:T(1,128)}, u32[]{:S(2)}) copy-start(s32[1,16]{1,0:T(1,128)} %param.14) | copy-start | bytes 196
  14.5 20.8 %copy-start.5 = (bf16[1024]{0:T(1024)(128)(2,1)S(1)}, bf16[1024]{0:T(1024)(128)(2,1)}, u32[]{:S(2)}) copy-start(bf16[1024]{0:T(1024)(128)(2,1)} %param.10) | copy-start | bytes 6148
  14.5 16.1 %collective-permute-start = (f32[128,1024]{1,0:T(8,128)}, f32[128,1024]{1,0:T(8,128)S(1)}, u32[]{:S(2)}, u32[]{:S(2)}) collective-permute-start(f32[128,1024]{1,0:T(8,128)} %bitcast.14), channel_id=1, source_target_pairs={{0,1},{1,0},{2,3},{3,2},{4,5},{5,4},{6,7},{7,6},{8,9},{9,8},{10,11... | collective-permute-start | bytes 1572872 | tf_op jit(solution)/shard_map/ppermute | solution.py:483
  21.3 20.5 %copy-start = (bf16[4,1,32,4096]{3,2,1,0:T(8,128)(2,1)S(1)}, bf16[4,1,32,4096]{3,2,1,0:T(8,128)(2,1)}, u32[]{:S(2)}) copy-start(bf16[4,1,32,4096]{3,2,1,0:T(8,128)(2,1)} %query_ref.5) | copy-start | bytes 3145732
  21.3 20.5 %copy-start.2 = (f32[1,128,1024]{2,1,0:T(8,128)S(1)}, f32[1,128,1024]{2,1,0:T(8,128)}, u32[]{:S(2)}) copy-start(f32[1,128,1024]{2,1,0:T(8,128)} %project.3) | copy-start | bytes 1572868
  30.7 19.3 %all-to-all-start.1 = ((bf16[16,136,128]{2,1,0:T(8,128)(2,1)}), bf16[16,136,128]{2,1,0:T(8,128)(2,1)S(1)}, u32[]{:S(2)}, u32[]{:S(2)}) async-start(bf16[16,136,128]{2,1,0:T(8,128)(2,1)} %moving_old.1), calls=%async_computation.1 | async-start | bytes 1114112 | tf_op jit(solution)/shard_map/all_to_all | solution.py:510
  41.8 1.1 %copy-start.1 = (bf16[16,136,128]{2,1,0:T(8,128)(2,1)S(1)}, bf16[16,136,128]{2,1,0:T(8,128)(2,1)}, u32[]{:S(2)}) copy-start(bf16[16,136,128]{2,1,0:T(8,128)(2,1)} %staying_old.1.old_ref) | copy-start | bytes 1671172
